TPU v7x, 512 devices: a whole 4x4x16 slice. The times are simulated.
512 devices in a mesh: hour: 8 (over y, z_hi), sta: 64 (over x, z_lo, core).
Axes of the slice: x: 4, y: 4, z: 16 (z_hi: 2, z_lo: 8; z = z_hi * 8 + z_lo), core: 2. Of those that a mesh axis runs over, the one named last changes fastest.
Arguments:
- records: bfloat16 [8, 1024, 8, 512], P('hour', 'sta'), may hold values from -6 to 6
- masks: int32 [8, 1024, 8], P('hour', 'sta'), may hold values 0 or 1
- plan: int32 [4], replicated, may hold values from 0 to 63
Outputs:
- stacks: bfloat16 [4, 1024, 16, 201], P(None, 'sta', 'hour')
All inputs are finite; a program needn't handle non-finite values. No bound on the sum of `masks` on one device may be relied on, other than what follows from the above.
Results may differ from a plain program's by a relative error of at most 0.0055.
Values may be sent and summed in bfloat16 or wider, within the bound.
No kernel may reach another device: no remote copies, remote signals or barrier semaphores. Data moves between devices by JAX's collectives and lax.ppermute only.
A program may use at most 64 MiB of HBM per device.

v0:
```python
import math

import jax
import jax.numpy as jnp
from jax import lax
from jax.sharding import PartitionSpec as P

FREQ = 256
LAGS = 201


def from_root(array, axis, root):
    mine = lax.axis_index(axis) == root
    return lax.psum(jnp.where(mine, array, jnp.zeros_like(array)), axis)


def band_matrix(length, reach):
    places = jnp.arange(length, dtype=jnp.int32)
    return (jnp.abs(places[:, None] - places[None, :]) <= reach).astype(jnp.float32)


def angle_table(first, second, length):
    product = first[:, None] * second[None, :] % length
    return 2.0 * math.pi * product.astype(jnp.float32) / length


def whiten(traces, valid, seglen, nfreq):
    rows = traces.shape[:-1]
    raw = traces.reshape(-1, seglen)
    signal = raw.astype(jnp.float32)
    band_time = band_matrix(seglen, seglen // 8)
    envelope = (
        jnp.dot(jnp.abs(raw), band_time.astype(jnp.bfloat16), preferred_element_type=jnp.float32)
        / jnp.sum(band_time, axis=0)
        + 1e-06
    )
    normed = signal / envelope
    angles = angle_table(
        jnp.arange(seglen, dtype=jnp.int32), jnp.arange(nfreq, dtype=jnp.int32), seglen
    )
    spec_re = jnp.dot(normed, jnp.cos(angles), precision=lax.Precision.HIGHEST)
    spec_im = -jnp.dot(normed, jnp.sin(angles), precision=lax.Precision.HIGHEST)
    magnitude = jnp.sqrt(spec_re * spec_re + spec_im * spec_im)
    band_freq = band_matrix(nfreq, nfreq // 4)
    smooth = (
        jnp.dot(magnitude, band_freq, precision=lax.Precision.HIGHEST) / jnp.sum(band_freq, axis=0)
        + 1e-06
    )
    weight = valid.astype(jnp.float32).reshape(-1, 1) / smooth
    white = jnp.stack([spec_re * weight, spec_im * weight])
    return white.reshape((2,) + rows + (nfreq,)).astype(jnp.bfloat16)


def lag_table(nfreq, seglen, nlags, scale):
    shifts = jnp.arange(nlags, dtype=jnp.int32) - nlags // 2
    angles = angle_table(jnp.arange(nfreq, dtype=jnp.int32), shifts, seglen)
    return jnp.concatenate([jnp.cos(angles), -jnp.sin(angles)], axis=0) * scale


def cross_lags(left, right, table):
    real = jnp.einsum("asf,bsf->abf", left[0], right[0], preferred_element_type=jnp.float32)
    real = real + jnp.einsum("asf,bsf->abf", left[1], right[1], preferred_element_type=jnp.float32)
    imag = jnp.einsum("asf,bsf->abf", left[1], right[0], preferred_element_type=jnp.float32)
    imag = imag - jnp.einsum("asf,bsf->abf", left[0], right[1], preferred_element_type=jnp.float32)
    count_a, count_b = (real.shape[0], real.shape[1])
    flat = jnp.concatenate([real, imag], axis=-1).reshape(count_a * count_b, -1)
    return jnp.dot(flat, table, precision=lax.Precision.HIGHEST).reshape(
        count_a, count_b, table.shape[1]
    )


def shards(records, masks, plan):
    seglen = records.shape[3]
    nsegs = records.shape[2]
    spectra = whiten(records[0], masks[0], seglen, FREQ)
    hour_count = lax.axis_size("hour")
    table = lag_table(FREQ, seglen, LAGS, 1.0 / math.sqrt(nsegs * FREQ * hour_count))
    results = []
    for section in range(plan.shape[0]):
        source = from_root(spectra, "sta", plan[section])
        lagged = cross_lags(spectra, source, table)
        results.append(lax.psum_scatter(lagged, "hour", scatter_dimension=1, tiled=True))
    stacked = jnp.stack(results)
    return stacked.astype(jnp.bfloat16)


def solution(mesh):
    placed = (P("hour", "sta", None, None), P("hour", "sta", None), P())
    return jax.shard_map(
        shards, mesh=mesh, in_specs=placed, out_specs=P(None, "sta", "hour", None), check_vma=False
    )
```

profile of v0, /device:TPU:1, one launch (start us, length us, event | category | flops | bytes accessed | tf_op | source)
XLA Modules:
  0.0 1313.2 jit_solution(15504809226528045897)
XLA Ops:
  9.0 2.5 fusion.16
  11.5 2.4 fusion.18
  21.0 828.4 %all-reduce.3.cloned.1.call-done = (bf16[2,16,8,256]{3,2,1,0:T(8,128)(2,1)}, bf16[2,16,8,256]{3,2,1,0:T(8,128)(2,1)}, bf16[2,16,8,256]{3,2,1,0:T(8,128)(2,1)}, bf16[2,16,8,256]{3,2,1,0:T(8,128)(2,1)}) async-done(((bf16[2,16,8,256]{3,2,1,0:T(8,128)(2,1)}, bf16[2,16,8,256]{3,2,1,0:T(8,128)(2,1)}, bf16[2,16,8,256]{3,2,1,0:T(8,128)(2,1)}, bf16[2,16,8,256]{3,2,1,0:T(8,128)(2,1)}), ...) | async-done | bytes 524304 | tf_op jit(solution)/shard_map/psum | solution.py:14
  851.3 1.9 fusion.66
  853.3 1.9 fusion.67
  856.3 1.9 fusion.64
  860.5 2.0 copy.147
  862.5 3.0 fusion.68
  865.5 1.9 fusion.69
  867.4 2.0 copy.138
  869.4 3.7 add_bitcast_fusion.2
  873.1 3.3 copy.144
  876.4 3.7 subtract_bitcast_fusion.2
  880.0 3.3 copy.145
  884.4 2.5 fusion.12
  888.3 3.7 add_bitcast_fusion.3
  891.9 3.3 copy.133
  895.2 2.9 subtract_bitcast_fusion.3
  898.1 3.4 copy.134
  902.7 3.0 add_bitcast_fusion.1
  905.8 1.9 subtract_bitcast_fusion.1
  909.3 1.8 copy.155
  911.1 3.2 copy.156
  918.2 2.5 fusion.10
  921.8 2.9 fusion.71
  925.1 3.0 add_bitcast_fusion
  928.1 1.9 subtract_bitcast_fusion
  931.1 2.6 copy.167
  935.4 57.7 %reduce-scatter.7.cloned.1.call-done = f32[16,2,201]{2,0,1:T(8,128)} async-done(((f32[16,16,201]{2,0,1:T(8,128)}), f32[16,2,201]{2,0,1:T(8,128)}) %reduce-scatter.7.cloned.1.call-update) | async-done | bytes 25744 | tf_op jit(solution)/shard_map/reduce_scatter | solution.py:82
  993.8 103.1 %reduce-scatter.5.cloned.1.call-done = f32[16,2,201]{2,0,1:T(8,128)} async-done(((f32[16,16,201]{2,0,1:T(8,128)}), f32[16,2,201]{2,0,1:T(8,128)}) %reduce-scatter.5.cloned.1.call-update) | async-done | bytes 25744 | tf_op jit(solution)/shard_map/reduce_scatter | solution.py:82
  1097.7 103.7 %reduce-scatter.9.cloned.1.call-done = f32[16,2,201]{2,0,1:T(8,128)} async-done(((f32[16,16,201]{2,0,1:T(8,128)}), f32[16,2,201]{2,0,1:T(8,128)}) %reduce-scatter.9.cloned.1.call-update) | async-done | bytes 25744 | tf_op jit(solution)/shard_map/reduce_scatter | solution.py:82
  1202.2 103.0 %reduce-scatter.11.cloned.1.call-done = f32[16,2,201]{2,0,1:T(8,128)} async-done(((f32[16,16,201]{2,0,1:T(8,128)}), f32[16,2,201]{2,0,1:T(8,128)}) %reduce-scatter.11.cloned.1.call-update) | async-done | bytes 25744 | tf_op jit(solution)/shard_map/reduce_scatter | solution.py:82
  (84 shorter events, 29.2 us)
Async XLA Ops:
  6.5 842.9 %all-reduce.3.cloned.1.call-start = ((), (), s32[]{:S(2)}) async-start(), calls=%async_computation.8 | async-start | bytes 1048576 | tf_op jit(solution)/shard_map/psum | solution.py:14
  9.0 5.0 copy-start.16
  9.0 8.1 copy-start.17
  18.4 974.6 %reduce-scatter.7.cloned.1.call-start = ((), (), s32[]{:S(2)}) async-start(), calls=%async_computation.5 | async-start | bytes 294912 | tf_op jit(solution)/shard_map/reduce_scatter | solution.py:82
  855.5 0.8 copy-start.9
  858.2 1.6 copy-start.14
  858.2 1.6 copy-start.15
  862.5 3.0 copy-start.10
  886.9 210.0 %reduce-scatter.5.cloned.1.call-start = ((), (), s32[]{:S(2)}) async-start(), calls=%async_computation.4 | async-start | bytes 294912 | tf_op jit(solution)/shard_map/reduce_scatter | solution.py:82
  898.1 3.4 copy-start.13
  898.1 4.5 copy-start.1
  902.7 3.0 copy-start
  902.7 3.0 copy-start.8
  905.7 1.9 copy-start.11
  905.7 1.9 copy-start.12
  905.7 2.0 copy-start.5
  907.6 1.7 copy-start.3
  917.1 284.4 %reduce-scatter.9.cloned.1.call-start = ((), (), s32[]{:S(2)}) async-start(), calls=%async_computation.6 | async-start | bytes 294912 | tf_op jit(solution)/shard_map/reduce_scatter | solution.py:82
  924.7 380.5 %reduce-scatter.11.cloned.1.call-start = ((), (), s32[]{:S(2)}) async-start(), calls=%async_computation.7 | async-start | bytes 294912 | tf_op jit(solution)/shard_map/reduce_scatter | solution.py:82
  925.0 3.1 copy-start.2
  925.0 3.1 copy-start.7
  928.1 1.9 copy-start.4
  931.1 2.7 copy-start.6
Sparse Core Ops, SparseCore 0:
  18.6 830.8 all-reduce.2
  887.0 105.9 reduce-scatter.6
  997.5 99.4 reduce-scatter.4
  1101.9 99.5 reduce-scatter.8
  1205.7 99.4 reduce-scatter.10
where the time goes:
time: 1310 us
  waiting for transfers between devices  1200 us (92%)
  matrix products  55 us (4%)
  local copies, waits for them, and re-layouts  36.5 us (3%)
  between operations  15.9 us (1%)
    psum x1, waiting for transfers between devices, from_root(): return lax.psum(jnp.where(mine, array, jnp.zeros_like(array)), axis)  828 us
    reduce_scatter x4, waiting for transfers between devices, shards(): lax.psum_scatter(lagged, 'hour', scatter_dimension=1, tiled=True)  368 us
  transfers between devices with their start and end apart: 5, of which 5 were waited for; matrix products, arithmetic and copies ran while one was open for 4% of the time, Pallas kernels for 0%

commit v1 on v0

v1 whole, which is shorter than its diff:
```python
import math

import jax
import jax.numpy as jnp
import numpy as np
from jax import lax
from jax.experimental import pallas as pl
from jax.experimental.pallas import tpu as pltpu
from jax.sharding import Mesh, PartitionSpec as P

SB = 16
NSEG = 8
SEGLEN = 512
FREQ = 256
LAGS = 201
STEPS = 4
HOURS = 8
ROWS = SB * NSEG
WIDE = 2 * FREQ
LANES = 128
PAD = 256
PIECE = 2 * NSEG
TILES = WIDE // LANES
GROUP = 32
LINES = 4
SLOTS = 2 * STEPS

F32 = jnp.float32
BF16 = jnp.bfloat16
VMEM_LIMIT = 16 * 1024 * 1024


def angle_rows(times):
    angles = 2.0 * math.pi * ((np.asarray(times)[:, None] * np.arange(FREQ)[None, :]) % SEGLEN) / SEGLEN
    return np.concatenate([np.cos(angles), -np.sin(angles)], axis=1).astype(np.float32)


def lag_tables():
    shifts = np.arange(LAGS) - LAGS // 2
    angles = 2.0 * math.pi * ((np.arange(FREQ)[:, None] * shifts[None, :]) % SEGLEN) / SEGLEN
    table = np.concatenate([np.cos(angles), -np.sin(angles)], axis=0) / math.sqrt(NSEG * FREQ * HOURS)
    table = np.pad(table, ((0, 0), (0, PAD - LAGS)))
    high = table.astype(BF16)
    return high, (table - high.astype(np.float64)).astype(BF16)


def mm(left, right):
    return jnp.dot(left, right, preferred_element_type=F32)


def split(value):
    high = value.astype(BF16)
    return high, (value - high.astype(F32)).astype(BF16)


def band(length, reach):
    first = lax.broadcasted_iota(jnp.int32, (length, length), 0)
    second = lax.broadcasted_iota(jnp.int32, (length, length), 1)
    matrix = jnp.where(jnp.abs(first - second) <= reach, 1.0, 0.0).astype(BF16)
    place = lax.broadcasted_iota(jnp.int32, (1, length), 1)
    count = jnp.minimum(place + reach, length - 1) - jnp.maximum(place - reach, 0) + 1
    return matrix, count.astype(F32)


def whiten_kernel(records, mask, first_rows, turns, white, raw_buffer, trig, sem):
    fetch = pltpu.make_async_copy(records, raw_buffer, sem)
    fetch.start()
    trig[pl.ds(0, NSEG), :] = first_rows[...]
    size, level = NSEG, 0
    while size < SEGLEN:
        cos, sin = trig[pl.ds(0, size), :FREQ], trig[pl.ds(0, size), FREQ:]
        turn_cos, turn_sin = turns[pl.ds(level, 1), :FREQ], turns[pl.ds(level, 1), FREQ:]
        trig[pl.ds(size, size), :FREQ] = cos * turn_cos - sin * turn_sin
        trig[pl.ds(size, size), FREQ:] = sin * turn_cos + cos * turn_sin
        size, level = 2 * size, level + 1
    table_high, table_low = split(trig[...])
    time_band, time_count = band(SEGLEN, SEGLEN // 8)
    freq_band, freq_count = band(FREQ, FREQ // 4)
    fetch.wait()
    raw = raw_buffer[...]
    envelope = mm(jnp.abs(raw), time_band) / time_count + 1e-06
    high, low = split(raw.astype(F32) / envelope)
    spec = mm(high, table_high) + (mm(low, table_high) + mm(high, table_low))
    spec_re, spec_im = spec[:, :FREQ], spec[:, FREQ:]
    magnitude = jnp.sqrt(spec_re * spec_re + spec_im * spec_im)
    high, low = split(magnitude)
    smooth = (mm(high, freq_band) + mm(low, freq_band)) / freq_count + 1e-06
    station = lax.broadcasted_iota(jnp.int32, (SB, NSEG, SB), 0)
    column = lax.broadcasted_iota(jnp.int32, (SB, NSEG, SB), 2)
    spread = jnp.where(station == column, mask[...].astype(F32)[None], 0.0)
    valid = jnp.sum(spread, axis=2, keepdims=True)
    weight = (valid / smooth.reshape(SB, NSEG, FREQ)).reshape(ROWS, FREQ)
    for tile in range(TILES):
        spec_part = (spec_re, spec_im)[tile // 2]
        lanes = slice((tile % 2) * LANES, (tile % 2 + 1) * LANES)
        part = (spec_part[:, lanes] * weight[:, lanes]).astype(BF16)
        for group in range(ROWS // PIECE):
            white[tile * (ROWS // PIECE) + group] = part[group * PIECE : (group + 1) * PIECE]


def whiten(records, masks):
    vmem = pl.BlockSpec(memory_space=pltpu.VMEM)
    return pl.pallas_call(
        whiten_kernel,
        in_specs=[pl.BlockSpec(memory_space=pltpu.HBM), vmem, vmem, vmem],
        out_specs=vmem,
        out_shape=jax.ShapeDtypeStruct((GROUP, PIECE, LANES), BF16),
        scratch_shapes=[
            pltpu.VMEM((ROWS, SEGLEN), BF16),
            pltpu.VMEM((SEGLEN, WIDE), F32),
            pltpu.SemaphoreType.DMA,
        ],
        compiler_params=pltpu.CompilerParams(vmem_limit_bytes=VMEM_LIMIT),
        name="whiten",
    )(records, masks, jnp.asarray(angle_rows(range(NSEG))), jnp.asarray(angle_rows([8, 16, 32, 64, 128, 256, 0, 0])))


def pick_block_kernel(plan, gathered, picked):
    for k in range(STEPS):
        block = plan[k]
        picked[k] = gathered[(block // 16) * 8 + block % 8]


def pick_block(plan, gathered):
    vmem = pl.BlockSpec(memory_space=pltpu.VMEM)
    return pl.pallas_call(
        pick_block_kernel,
        in_specs=[pl.BlockSpec(memory_space=pltpu.SMEM), vmem],
        out_specs=vmem,
        out_shape=jax.ShapeDtypeStruct((STEPS, PIECE, LANES), BF16),
        compiler_params=pltpu.CompilerParams(vmem_limit_bytes=VMEM_LIMIT),
        name="pick_block",
    )(plan, gathered)


def pick_end_kernel(plan, end, mine, other, spread):
    for k in range(STEPS):
        here = (plan[k] // 8) % 2 == end[0]
        piece = jnp.where(here, mine[k].astype(F32), other[k].astype(F32)).astype(BF16)
        for to in range(GROUP // 2):
            spread[to, k] = piece


def pick_end(plan, end, mine, other):
    vmem = pl.BlockSpec(memory_space=pltpu.VMEM)
    smem = pl.BlockSpec(memory_space=pltpu.SMEM)
    return pl.pallas_call(
        pick_end_kernel,
        in_specs=[smem, smem, vmem, vmem],
        out_specs=vmem,
        out_shape=jax.ShapeDtypeStruct((GROUP // 2, STEPS, PIECE, LANES), BF16),
        compiler_params=pltpu.CompilerParams(vmem_limit_bytes=VMEM_LIMIT),
        name="pick_end",
    )(plan, end, mine, other)


def correlate_pairs(core, white, source, table_high, table_low, lagged, own, wide, cross):
    for tile in range(TILES):
        own[tile] = white[pl.ds(tile * 8, 8)].astype(F32).reshape(ROWS, LANES)
        wide[tile] = source[pl.ds(tile * LINES, LINES)].astype(F32).reshape(LINES * STEPS * PIECE, LANES)

    def pair(line, carry):
        for half in range(2):
            right = []
            for s in range(NSEG):
                rows = pl.ds(line * (STEPS * PIECE) + s, SLOTS, stride=NSEG)
                right.append((wide[half, rows, :], wide[half + 2, rows, :]))
            for a in range(SB):
                real = imag = None
                for s in range(NSEG):
                    row = pl.ds(a * NSEG + s, 1)
                    left_re = jnp.broadcast_to(own[half, row, :], (SLOTS, LANES))
                    left_im = jnp.broadcast_to(own[half + 2, row, :], (SLOTS, LANES))
                    right_re, right_im = right[s]
                    add_re = left_re * right_re + left_im * right_im
                    add_im = left_im * right_re - left_re * right_im
                    real = add_re if s == 0 else real + add_re
                    imag = add_im if s == 0 else imag + add_im
                cross[pl.ds(a * SLOTS, SLOTS), pl.ds(half * LANES, LANES)] = real
                cross[pl.ds(a * SLOTS, SLOTS), pl.ds(FREQ + half * LANES, LANES)] = imag
        high, low = split(cross[...])
        out = mm(high, table_high[...]) + (mm(low, table_high[...]) + mm(high, table_low[...]))
        lagged[line * 2 + core] = out.astype(BF16)
        return carry

    lax.fori_loop(0, LINES, pair, 0)


def correlate_near_kernel(core, white, source, table_high, table_low, lagged, own, wide, cross):
    correlate_pairs(core[0], white, source, table_high, table_low, lagged, own, wide, cross)


def correlate_far_kernel(core, near, white, source, table_high, table_low, lagged, own, wide, cross):
    for line in range(LINES):
        lagged[line * 2 + core[0]] = near[line * 2 + core[0]]
    correlate_pairs(1 - core[0], white, source, table_high, table_low, lagged, own, wide, cross)


def correlate(kernel, name, core, *arrays):
    vmem = pl.BlockSpec(memory_space=pltpu.VMEM)
    arrays = arrays + tuple(jnp.asarray(t) for t in lag_tables())
    return pl.pallas_call(
        kernel,
        in_specs=[pl.BlockSpec(memory_space=pltpu.SMEM)] + [vmem] * len(arrays),
        out_specs=vmem,
        out_shape=jax.ShapeDtypeStruct((HOURS, ROWS, PAD), BF16),
        scratch_shapes=[
            pltpu.VMEM((TILES, ROWS, LANES), F32),
            pltpu.VMEM((TILES, LINES * STEPS * PIECE, LANES), F32),
            pltpu.VMEM((ROWS, WIDE), F32),
        ],
        compiler_params=pltpu.CompilerParams(vmem_limit_bytes=VMEM_LIMIT),
        name=name,
    )(core, *arrays)


def shards(records, masks, plan):
    core = lax.axis_index("c").astype(jnp.int32).reshape(1)
    end = lax.axis_index("u").astype(jnp.int32).reshape(1)
    white = whiten(records.reshape(ROWS, SEGLEN), masks[0].T)
    pieces = lax.all_to_all(white, ("x", "v", "c"), 0, 0, tiled=True)
    mine = pick_block(plan, pieces)
    other = lax.ppermute(mine, "u", [(0, 1), (1, 0)])
    spread = pick_end(plan, end, mine, other)
    near = lax.all_to_all(spread, ("x", "v"), 0, 0, tiled=True)
    far = lax.ppermute(near, "c", [(0, 1), (1, 0)])
    lagged = correlate(correlate_near_kernel, "correlate_near", core, white, near)
    lagged = correlate(correlate_far_kernel, "correlate_far", core, lagged, white, far)
    parts = lax.all_to_all(lagged, ("y", "w"), 0, 0, tiled=True)
    total = jnp.sum(parts.astype(F32), axis=0).astype(BF16)
    total = total[:, :LAGS].reshape(SB, STEPS, 2, LAGS)
    return jnp.transpose(total, (1, 0, 2, 3))


def solution(mesh):
    grid = Mesh(mesh.devices.reshape(4, 2, 4, 2, 4, 2), ("y", "w", "x", "u", "v", "c"))
    hour = ("y", "w")
    sta = ("x", "u", "v", "c")
    return jax.shard_map(
        shards,
        mesh=grid,
        in_specs=(P(hour, sta, None, None), P(hour, sta, None), P()),
        out_specs=P(None, sta, hour, None),
        check_vma=False,
    )
```

time: 1310 us -> 103 us (0.08)
  the two profiles are of different devices: /device:TPU:1 before, /device:TPU:33 now
where the time goes in v1:
time: 103 us; the launch traced here: 102 us
  blocking collectives  77.5 us (75%)
  starting transfers between devices  12.5 us (12%)
  Pallas kernels  6.68 us (6%)
  local copies, waits for them, and re-layouts  3.77 us (4%)
  waiting for transfers between devices  1.58 us (2%)
    all_to_all x1, blocking collectives, shards(): parts = lax.all_to_all(lagged, ('y', 'w'), 0, 0, tiled=True)  47.8 us
    all_to_all x1, blocking collectives, shards(): pieces = lax.all_to_all(white, ('x', 'v', 'c'), 0, 0, tiled=True)  16.3 us
    all_to_all x1, blocking collectives, shards(): near = lax.all_to_all(spread, ('x', 'v'), 0, 0, tiled=True)  13.4 us
    ppermute x1, starting transfers between devices, shards(): other = lax.ppermute(mine, 'u', [(0, 1), (1, 0)])  8.84 us
    pallas_call x2, Pallas kernels, correlate(): pl.pallas_call(kernel, in_specs=[pl.BlockSpec(memory_space=pltpu.SMEM)] +...  4.28 us
    ppermute x1, starting transfers between devices, shards(): far = lax.ppermute(near, 'c', [(0, 1), (1, 0)])  3.64 us
    unnamed x14, local copies, waits for them, and re-layouts  3.04 us
  transfers between devices with their start and end apart: 2, of which 1 were waited for; matrix products, arithmetic and copies ran while one was open for 0% of the time, Pallas kernels for 2%

profile of v1, /device:TPU:33, one launch (start us, length us, event | category | flops | bytes accessed | tf_op | source)
XLA Modules:
  0.0 102.2 jit_solution(10997602868945982767)
XLA Ops:
  0.0 0.0 copy-start.2
  0.0 0.9 copy-done.2
  0.9 0.0 copy-start.3
  0.9 0.7 copy-done.3
  1.6 0.0 copy-start.4
  1.6 0.7 copy-done.4
  2.3 0.0 copy-start.5
  2.3 0.7 copy-done.5
  3.0 1.2 %whiten.1.white = bf16[32,16,128]{2,1,0:T(8,128)(2,1)S(1)} custom-call(bf16[128,512]{1,0:T(8,128)(2,1)S(1)} %bitcast.8, s32[8,16]{1,0:T(8,128)S(1)} %bitcast.9, f32[8,512]{1,0:T(8,128)S(1)} %copy-done.4, f32[8,512]{1,0:T(8,128)S(1)} %copy-done.3), custom_call_target="tpu_custom_call" | custom-call | tf_op jit(solution)/shard_map/whiten/pallas_call | solution.py:103
  4.3 0.0 copy-start.6
  4.3 16.3 %all_to_all.15.gathered = bf16[32,16,128]{2,1,0:T(8,128)(2,1)S(1)} all-to-all(bf16[32,16,128]{2,1,0:T(8,128)(2,1)S(1)} %whiten.1.white), channel_id=1, replica_groups=mesh['y'=4,'w'=2,'x'=4,'u'=2,'v'=4,'c'=2] {'x','v','c'}, dimensions={0} | all-to-all | bytes 262144 | tf_op jit(solution)/shard_map/all_to_all | solution.py:221
  20.6 0.0 copy-done.6
  20.6 0.6 pick_block.1.mine
  21.2 8.8 %collective-permute-start = (bf16[4,16,128]{2,1,0:T(8,128)(2,1)S(1)}, bf16[4,16,128]{2,1,0:T(8,128)(2,1)S(1)}, u32[]{:S(2)}, u32[]{:S(2)}) collective-permute-start(bf16[4,16,128]{2,1,0:T(8,128)(2,1)S(1)} %pick_block.1.mine), channel_id=1, source_target_pairs={{0,8},{8,0},{1,9},{9,1},{2,10},{10,2},{3,11},{11,3},{4,12},{12,4},... | collective-permute-start | bytes 49160 | tf_op jit(solution)/shard_map/ppermute | solution.py:223
  30.0 1.6 %collective-permute-done.other = bf16[4,16,128]{2,1,0:T(8,128)(2,1)S(1)} collective-permute-done((bf16[4,16,128]{2,1,0:T(8,128)(2,1)S(1)}, bf16[4,16,128]{2,1,0:T(8,128)(2,1)S(1)}, u32[]{:S(2)}, u32[]{:S(2)}) %collective-permute-start) | collective-permute-done | bytes 16416 | tf_op jit(solution)/shard_map/ppermute | solution.py:223
  31.6 0.6 pick_end.1
  32.2 0.0 copy-start
  32.2 0.0 copy-start.1
  32.2 13.4 %all_to_all.16.source = bf16[16,4,16,128]{3,2,1,0:T(8,128)(2,1)S(1)} all-to-all(bf16[16,4,16,128]{3,2,1,0:T(8,128)(2,1)S(1)} %pick_end.1), channel_id=1, replica_groups=mesh['y'=4,'w'=2,'x'=4,'u'=2,'v'=4,'c'=2] {'x','v'}, dimensions={0} | all-to-all | bytes 524288 | tf_op jit(solution)/shard_map/all_to_all | solution.py:225
  45.6 3.6 %collective-permute-start.1 = (bf16[16,4,16,128]{3,2,1,0:T(8,128)(2,1)S(1)}, bf16[16,4,16,128]{3,2,1,0:T(8,128)(2,1)S(1)}, u32[]{:S(2)}, u32[]{:S(2)}) collective-permute-start(bf16[16,4,16,128]{3,2,1,0:T(8,128)(2,1)S(1)} %all_to_all.16.source), channel_id=1, source_target_pairs={{0,1},{1,0},{2,3},{3,2},{4,5},{5,4},{6,7},{7,6},{8,9},{9,8},{10,11... | collective-permute-start | bytes 786440 | tf_op jit(solution)/shard_map/ppermute | solution.py:226
  49.3 0.0 copy-done
  49.3 0.0 copy-done.1
  49.3 2.1 %correlate_near.1.near = bf16[8,128,256]{2,1,0:T(8,128)(2,1)S(1)} custom-call(s32[1]{0:T(128)} %bitcast.core, bf16[32,16,128]{2,1,0:T(8,128)(2,1)S(1)} %whiten.1.white, bf16[16,4,16,128]{3,2,1,0:T(8,128)(2,1)S(1)} %all_to_all.16.source, bf16[512,256]{1,0:T(8,128)(2,1)S(1)} %copy-done.1, bf16[512,256]{1,0:T(8,128)(2,1)S(1)} %copy-done), custom_call_target="tpu_custom_call" | custom-call | tf_op jit(solution)/shard_map/correlate_near/pallas_call | solution.py:202
  51.4 0.0 collective-permute-done.1.source
  51.4 2.1 %correlate_far.1 = bf16[8,128,256]{2,1,0:T(8,128)(2,1)S(1)} custom-call(s32[1]{0:T(128)} %bitcast.core, bf16[8,128,256]{2,1,0:T(8,128)(2,1)S(1)} %correlate_near.1.near, bf16[32,16,128]{2,1,0:T(8,128)(2,1)S(1)} %whiten.1.white, bf16[16,4,16,128]{3,2,1,0:T(8,128)(2,1)S(1)} %collective-permute-done.1.source, bf16[512,256]{1,0:T(8,128)(2,1)S(1)} %copy-done.1, ...), custom_call_target="tpu_custom_call" | custom-call | tf_op jit(solution)/shard_map/correlate_far/pallas_call | solution.py:202
  53.6 47.8 %all_to_all.17 = bf16[8,128,256]{2,1,0:T(8,128)(2,1)S(1)} all-to-all(bf16[8,128,256]{2,1,0:T(8,128)(2,1)S(1)} %correlate_far.1), channel_id=1, replica_groups=mesh['y'=4,'w'=2,'x'=4,'u'=2,'v'=4,'c'=2] {'y','w'}, dimensions={0} | all-to-all | bytes 1048576 | tf_op jit(solution)/shard_map/all_to_all | solution.py:229
  101.4 0.1 reduce_sum.12
  101.5 0.7 copy.10
  (1 shorter events, 0.0 us)
Async XLA Ops:
  0.0 0.9 copy-start.2
  0.9 0.7 copy-start.3
  1.6 0.7 copy-start.4
  2.3 0.7 copy-start.5
  4.3 16.3 %copy-start.6 = (s32[4]{0:T(128)S(1)}, s32[4]{0:T(128)}, u32[]{:S(2)}) copy-start(s32[4]{0:T(128)} %plan.3) | copy-start | bytes 52
  21.2 10.4 %collective-permute-start = (bf16[4,16,128]{2,1,0:T(8,128)(2,1)S(1)}, bf16[4,16,128]{2,1,0:T(8,128)(2,1)S(1)}, u32[]{:S(2)}, u32[]{:S(2)}) collective-permute-start(bf16[4,16,128]{2,1,0:T(8,128)(2,1)S(1)} %pick_block.1.mine), channel_id=1, source_target_pairs={{0,8},{8,0},{1,9},{9,1},{2,10},{10,2},{3,11},{11,3},{4,12},{12,4},... | collective-permute-start | bytes 49160 | tf_op jit(solution)/shard_map/ppermute | solution.py:223
  32.2 17.1 %copy-start = (bf16[512,256]{1,0:T(8,128)(2,1)S(1)}, bf16[512,256]{1,0:T(8,128)(2,1)}, u32[]{:S(2)}) copy-start(bf16[512,256]{1,0:T(8,128)(2,1)} %constant.22.clone.table_low) | copy-start | bytes 786436
  32.2 17.1 %copy-start.1 = (bf16[512,256]{1,0:T(8,128)(2,1)S(1)}, bf16[512,256]{1,0:T(8,128)(2,1)}, u32[]{:S(2)}) copy-start(bf16[512,256]{1,0:T(8,128)(2,1)} %constant.21.clone.table_high) | copy-start | bytes 786436
  45.6 5.8 %collective-permute-start.1 = (bf16[16,4,16,128]{3,2,1,0:T(8,128)(2,1)S(1)}, bf16[16,4,16,128]{3,2,1,0:T(8,128)(2,1)S(1)}, u32[]{:S(2)}, u32[]{:S(2)}) collective-permute-start(bf16[16,4,16,128]{3,2,1,0:T(8,128)(2,1)S(1)} %all_to_all.16.source), channel_id=1, source_target_pairs={{0,1},{1,0},{2,3},{3,2},{4,5},{5,4},{6,7},{7,6},{8,9},{9,8},{10,11... | collective-permute-start | bytes 786440 | tf_op jit(solution)/shard_map/ppermute | solution.py:226

commit v2 on v1

v2 whole, which is shorter than its diff:
```python
import math

import jax
import jax.numpy as jnp
import numpy as np
from jax import lax
from jax.experimental import pallas as pl
from jax.experimental.pallas import tpu as pltpu
from jax.sharding import Mesh, PartitionSpec as P

SB = 16
NSEG = 8
SEGLEN = 512
FREQ = 256
LAGS = 201
STEPS = 4
HOURS = 8
ROWS = SB * NSEG
WIDE = 2 * FREQ
LANES = 128
PIECE = 2 * NSEG
TILES = WIDE // LANES
UNITS = 32
LINES = 4
SPREAD = 16
SLOTS = 2 * STEPS
KEPT = 208

F32 = jnp.float32
BF16 = jnp.bfloat16
VMEM_LIMIT = 16 * 1024 * 1024


def angle_rows(times):
    product = (times * lax.broadcasted_iota(jnp.int32, times.shape, 1)) % SEGLEN
    angles = product.astype(F32) * (2.0 * math.pi / SEGLEN)
    return jnp.cos(angles), -jnp.sin(angles)


def lag_tables():
    shifts = np.arange(LAGS) - LAGS // 2
    angles = 2.0 * math.pi * ((shifts[:, None] * np.arange(FREQ)[None, :]) % SEGLEN) / SEGLEN
    table = np.concatenate([np.cos(angles), -np.sin(angles)], axis=1) / math.sqrt(NSEG * FREQ * HOURS)
    table = np.pad(table, ((0, KEPT - LAGS), (0, 0)))
    high = table.astype(BF16)
    return np.concatenate([high, (table - high.astype(np.float64)).astype(BF16)], axis=0)


def mm(left, right):
    return jnp.dot(left, right, preferred_element_type=F32)


def mm_rows(left, right):
    return lax.dot_general(left, right, (((1,), (1,)), ((), ())), preferred_element_type=F32)


def split(value):
    high = value.astype(BF16)
    return high, (value - high.astype(F32)).astype(BF16)


def band(length, reach):
    first = lax.broadcasted_iota(jnp.int32, (length, length), 0)
    second = lax.broadcasted_iota(jnp.int32, (length, length), 1)
    matrix = jnp.where(jnp.abs(first - second) <= reach, 1.0, 0.0).astype(BF16)
    place = lax.broadcasted_iota(jnp.int32, (1, length), 1)
    count = jnp.minimum(place + reach, length - 1) - jnp.maximum(place - reach, 0) + 1
    return matrix, count.astype(F32)


def whiten_kernel(records, mask, white, raw_buffer, mask_buffer, trig, sems):
    fetches = [
        pltpu.make_async_copy(records, raw_buffer, sems.at[0]),
        pltpu.make_async_copy(mask, mask_buffer, sems.at[1]),
    ]
    for fetch in fetches:
        fetch.start()
    row = lax.broadcasted_iota(jnp.int32, (NSEG, FREQ), 0)
    cos, sin = angle_rows(row)
    turns_cos, turns_sin = angle_rows(lax.shift_left(jnp.full_like(row, NSEG), row))
    trig[pl.ds(0, NSEG), :FREQ] = cos
    trig[pl.ds(0, NSEG), FREQ:] = sin
    size, level = NSEG, 0
    while size < SEGLEN:
        cos, sin = trig[pl.ds(0, size), :FREQ], trig[pl.ds(0, size), FREQ:]
        turn_cos, turn_sin = turns_cos[level : level + 1], turns_sin[level : level + 1]
        trig[pl.ds(size, size), :FREQ] = cos * turn_cos - sin * turn_sin
        trig[pl.ds(size, size), FREQ:] = sin * turn_cos + cos * turn_sin
        size, level = 2 * size, level + 1
    table_high, table_low = split(trig[...])
    time_band, time_count = band(SEGLEN, SEGLEN // 8)
    freq_band, freq_count = band(FREQ, FREQ // 4)
    for fetch in fetches:
        fetch.wait()
    raw = raw_buffer[...]
    envelope = mm(jnp.abs(raw), time_band) / time_count + 1e-06
    high, low = split(raw.astype(F32) / envelope)
    spec = mm(high, table_high) + (mm(low, table_high) + mm(high, table_low))
    spec_re, spec_im = spec[:, :FREQ], spec[:, FREQ:]
    magnitude = jnp.sqrt(spec_re * spec_re + spec_im * spec_im)
    high, low = split(magnitude)
    smooth = (mm(high, freq_band) + mm(low, freq_band)) / freq_count + 1e-06
    station = lax.broadcasted_iota(jnp.int32, (SB, NSEG, SB), 0)
    column = lax.broadcasted_iota(jnp.int32, (SB, NSEG, SB), 2)
    spread = jnp.where(station == column, mask_buffer[...].astype(F32)[None], 0.0)
    valid = jnp.sum(spread, axis=2, keepdims=True)
    weight = (valid / smooth.reshape(SB, NSEG, FREQ)).reshape(ROWS, FREQ)
    for tile in range(TILES):
        spec_part = (spec_re, spec_im)[tile // 2]
        lanes = slice((tile % 2) * LANES, (tile % 2 + 1) * LANES)
        part = (spec_part[:, lanes] * weight[:, lanes]).astype(BF16)
        for group in range(ROWS // PIECE):
            white[tile * (ROWS // PIECE) + group] = part[group * PIECE : (group + 1) * PIECE]


def whiten(records, masks):
    hbm = pl.BlockSpec(memory_space=pltpu.HBM)
    return pl.pallas_call(
        whiten_kernel,
        in_specs=[hbm, hbm],
        out_specs=pl.BlockSpec(memory_space=pltpu.VMEM),
        out_shape=jax.ShapeDtypeStruct((UNITS, PIECE, LANES), BF16),
        scratch_shapes=[
            pltpu.VMEM((ROWS, SEGLEN), BF16),
            pltpu.VMEM((NSEG, SB), jnp.int32),
            pltpu.VMEM((SEGLEN, WIDE), F32),
            pltpu.SemaphoreType.DMA((2,)),
        ],
        compiler_params=pltpu.CompilerParams(vmem_limit_bytes=VMEM_LIMIT),
        name="whiten",
    )(records, masks)


def pick_near_kernel(plan, gathered, picked):
    for k in range(STEPS):
        block = plan[k]
        picked[k] = gathered[(block // 16) * 8 + block % 8]


def pick_far_kernel(plan, gathered, spread):
    for k in range(STEPS):
        piece = gathered[(plan[k] // 8) % 2, k]
        for to in range(SPREAD):
            spread[to, k] = piece


def pick(kernel, plan, gathered, shape, name):
    vmem = pl.BlockSpec(memory_space=pltpu.VMEM)
    return pl.pallas_call(
        kernel,
        in_specs=[pl.BlockSpec(memory_space=pltpu.SMEM), vmem],
        out_specs=vmem,
        out_shape=jax.ShapeDtypeStruct(shape, BF16),
        compiler_params=pltpu.CompilerParams(vmem_limit_bytes=VMEM_LIMIT),
        name=name,
    )(plan, gathered)


def correlate_half(core, white, source, table, lagged, own, wide, cross):
    for tile in range(TILES):
        own[tile] = white[pl.ds(tile * 8, 8)].astype(F32).reshape(ROWS, LANES)
        wide[tile] = source[pl.ds(tile * LINES, LINES)].astype(F32).reshape(LINES * STEPS * PIECE, LANES)

    def pair(first, carry):
        for part in range(2):
            line = first * 2 + part
            for half in range(2):
                right = []
                for s in range(NSEG):
                    rows = pl.ds(line * (STEPS * PIECE) + s, SLOTS, stride=NSEG)
                    right.append((wide[half, rows, :], wide[half + 2, rows, :]))
                for a in range(SB):
                    real = imag = None
                    for s in range(NSEG):
                        row = pl.ds(a * NSEG + s, 1)
                        left_re = jnp.broadcast_to(own[half, row, :], (SLOTS, LANES))
                        left_im = jnp.broadcast_to(own[half + 2, row, :], (SLOTS, LANES))
                        right_re, right_im = right[s]
                        add_re = left_re * right_re + left_im * right_im
                        add_im = left_im * right_re - left_re * right_im
                        real = add_re if s == 0 else real + add_re
                        imag = add_im if s == 0 else imag + add_im
                    rows = pl.ds(part * ROWS + a * SLOTS, SLOTS)
                    cross[rows, pl.ds(half * LANES, LANES)] = real
                    cross[rows, pl.ds(FREQ + half * LANES, LANES)] = imag
        high, low = split(cross[...])
        both = mm_rows(table[...], high)
        out = (both[:KEPT] + (both[KEPT:] + mm_rows(table[pl.ds(0, KEPT), :], low))).astype(BF16)
        for part in range(2):
            lagged[first * 2 + part, core] = out[:, part * ROWS : (part + 1) * ROWS]
        return carry

    lax.fori_loop(0, LINES // 2, pair, 0)


def correlate_near_kernel(place, *refs):
    correlate_half(place[0], *refs)


def correlate_far_kernel(place, near, *refs):
    lagged = refs[3]
    for line in range(LINES):
        lagged[line, place[0]] = near[line, place[0]]
    correlate_half(1 - place[0], *refs)


def correlate(kernel, name, place, *arrays):
    vmem = pl.BlockSpec(memory_space=pltpu.VMEM)
    arrays = arrays + (jnp.asarray(lag_tables()),)
    return pl.pallas_call(
        kernel,
        in_specs=[pl.BlockSpec(memory_space=pltpu.SMEM)] + [vmem] * len(arrays),
        out_specs=vmem,
        out_shape=jax.ShapeDtypeStruct((LINES, 2, KEPT, ROWS), BF16),
        scratch_shapes=[
            pltpu.VMEM((TILES, ROWS, LANES), F32),
            pltpu.VMEM((TILES, LINES * STEPS * PIECE, LANES), F32),
            pltpu.VMEM((2 * ROWS, WIDE), F32),
        ],
        compiler_params=pltpu.CompilerParams(vmem_limit_bytes=VMEM_LIMIT),
        name=name,
    )(place, *arrays)


def fold_kernel(place, parts, keep, send):
    mine, other = place[1], 1 - place[1]
    keep_sum, send_sum = parts[0, mine].astype(F32), parts[0, other].astype(F32)
    for quad in range(1, LINES):
        keep_sum = keep_sum + parts[quad, mine].astype(F32)
        send_sum = send_sum + parts[quad, other].astype(F32)
    keep[...] = keep_sum
    send[...] = send_sum.astype(BF16)


def fold(place, parts):
    vmem = pl.BlockSpec(memory_space=pltpu.VMEM)
    return pl.pallas_call(
        fold_kernel,
        in_specs=[pl.BlockSpec(memory_space=pltpu.SMEM), vmem],
        out_specs=[vmem, vmem],
        out_shape=[jax.ShapeDtypeStruct((KEPT, ROWS), F32), jax.ShapeDtypeStruct((KEPT, ROWS), BF16)],
        compiler_params=pltpu.CompilerParams(vmem_limit_bytes=VMEM_LIMIT),
        name="fold",
    )(place, parts)


def finish_kernel(place, keep, both, out):
    total = (keep[...] + both[1 - place[1]].astype(F32)).astype(BF16)
    row = lax.broadcasted_iota(jnp.int32, (ROWS, ROWS), 0)
    column = lax.broadcasted_iota(jnp.int32, (ROWS, ROWS), 1)
    station, slot = (row // 2) % SB, (row // (2 * SB)) * 2 + row % 2
    order = jnp.where(column == station * SLOTS + slot, 1.0, 0.0).astype(BF16)
    out[...] = mm_rows(order, total)[:, :LAGS].astype(BF16)


def finish(place, keep, both):
    vmem = pl.BlockSpec(memory_space=pltpu.VMEM)
    return pl.pallas_call(
        finish_kernel,
        in_specs=[pl.BlockSpec(memory_space=pltpu.SMEM), vmem, vmem],
        out_specs=vmem,
        out_shape=jax.ShapeDtypeStruct((ROWS, LAGS), BF16),
        compiler_params=pltpu.CompilerParams(vmem_limit_bytes=VMEM_LIMIT),
        name="finish",
    )(place, keep, both)


def shards(records, masks, plan):
    place = jnp.stack([lax.axis_index("c"), lax.axis_index("w")]).astype(jnp.int32)
    white = whiten(records.reshape(ROWS, SEGLEN), masks[0].T)
    pieces = lax.all_to_all(white, ("x", "q", "r", "c"), 0, 0, tiled=True)
    picked = pick(pick_near_kernel, plan, pieces, (STEPS, PIECE, LANES), "pick_near")
    ends = lax.all_gather(picked, "p", axis=0, tiled=False)
    spread = pick(pick_far_kernel, plan, ends, (SPREAD, STEPS, PIECE, LANES), "pick_far")
    near = lax.all_to_all(spread, ("x", "q", "r"), 0, 0, tiled=True)
    far = lax.ppermute(near, "c", [(0, 1), (1, 0)])
    lagged = correlate(correlate_near_kernel, "correlate_near", place, white, near)
    lagged = correlate(correlate_far_kernel, "correlate_far", place, lagged, white, far)
    parts = lax.all_to_all(lagged, "y", 0, 0, tiled=True)
    keep, send = fold(place, parts)
    both = lax.all_gather(send, "w", axis=0, tiled=False)
    return finish(place, keep, both).reshape(STEPS, SB, 2, LAGS)


def solution(mesh):
    grid = Mesh(mesh.devices.reshape(4, 2, 4, 2, 2, 2, 2), ("y", "w", "x", "p", "q", "r", "c"))
    hour = ("y", "w")
    sta = ("x", "p", "q", "r", "c")
    return jax.shard_map(
        shards,
        mesh=grid,
        in_specs=(P(hour, sta, None, None), P(hour, sta, None), P()),
        out_specs=P(None, sta, hour, None),
        check_vma=False,
    )
```

time: 103 us -> 80.6 us (0.78)
  the two profiles are of different devices: /device:TPU:33 before, /device:TPU:1 now
where the time goes in v2:
time: 80.6 us; the launch traced here: 80.4 us
  blocking collectives  65.6 us (81%)
  Pallas kernels  8.56 us (11%)
  starting transfers between devices  3.75 us (5%)
  local copies, waits for them, and re-layouts  2.28 us (3%)
    all_to_all x1, blocking collectives, shards(): pieces = lax.all_to_all(white, ('x', 'q', 'r', 'c'), 0, 0, tiled=True)  18.5 us
    all_to_all x1, blocking collectives, shards(): near = lax.all_to_all(spread, ('x', 'q', 'r'), 0, 0, tiled=True)  12.6 us
    all_gather x1, blocking collectives, shards(): both = lax.all_gather(send, 'w', axis=0, tiled=False)  12.5 us
    all_to_all x1, blocking collectives, shards(): parts = lax.all_to_all(lagged, 'y', 0, 0, tiled=True)  12 us
    all_gather x1, blocking collectives, shards(): ends = lax.all_gather(picked, 'p', axis=0, tiled=False)  10.1 us
    pallas_call x2, Pallas kernels, correlate(): pl.pallas_call(kernel, in_specs=[pl.BlockSpec(memory_space=pltpu.SMEM)] +...  4.73 us
    ppermute x1, starting transfers between devices, shards(): far = lax.ppermute(near, 'c', [(0, 1), (1, 0)])  3.75 us
  transfers between devices with their start and end apart: 1, of which 0 were waited for; matrix products, arithmetic and copies ran while one was open for 0% of the time, Pallas kernels for 3%

profile of v2, /device:TPU:1, one launch (start us, length us, event | category | flops | bytes accessed | tf_op | source)
XLA Modules:
  0.0 80.4 jit_solution(6452975115683862332)
XLA Ops:
  0.0 0.0 copy-start.1
  0.0 0.9 %copy-done.1 = bf16[1,16,8,512]{3,2,1,0:T(8,128)(2,1)S(1)} copy-done((bf16[1,16,8,512]{3,2,1,0:T(8,128)(2,1)S(1)}, bf16[1,16,8,512]{3,2,1,0:T(8,128)(2,1)}, u32[]{:S(2)}) %copy-start.1) | copy-done | bytes 131096
  0.9 0.0 copy-start.2
  0.9 0.7 copy-done.2
  1.6 1.3 %whiten.1.refs_0_ = bf16[32,16,128]{2,1,0:T(8,128)(2,1)S(1)} custom-call(bf16[128,512]{1,0:T(8,128)(2,1)S(1)} %bitcast.10, s32[8,16]{1,0:T(8,128)S(1)} %bitcast.11), custom_call_target="tpu_custom_call" | custom-call | tf_op jit(solution)/shard_map/whiten/pallas_call | solution.py:118
  2.9 0.0 copy-start.3
  2.9 18.5 %all_to_all.15.gathered = bf16[32,16,128]{2,1,0:T(8,128)(2,1)S(1)} all-to-all(bf16[32,16,128]{2,1,0:T(8,128)(2,1)S(1)} %whiten.1.refs_0_), channel_id=1, replica_groups=mesh['y'=4,'w'=2,'x'=4,'p'=2,'q'=2,'r'=2,'c'=2] {'x','q','r','c'}, dimensions={0} | all-to-all | bytes 262144 | tf_op jit(solution)/shard_map/all_to_all | solution.py:271
  21.5 0.0 copy-done.3
  21.5 0.6 pick_near.1
  22.1 10.1 %all-gather = bf16[8,16,128]{2,1,0:T(8,128)(2,1)S(1)} all-gather(bf16[4,16,128]{2,1,0:T(8,128)(2,1)S(1)} %pick_near.1), channel_id=2, replica_groups=mesh['y'=4,'w'=2,'x'=4,'p'=2,'q'=2,'r'=2,'c'=2] {'p'}, dimensions={0}, use_global_device_ids=true | all-gather | bytes 49152 | tf_op jit(solution)/shard_map/all_gather | solution.py:273
  32.1 0.0 copy-start
  32.1 0.6 pick_far.1
  32.7 12.6 %all_to_all.16.refs_1_ = bf16[16,4,16,128]{3,2,1,0:T(8,128)(2,1)S(1)} all-to-all(bf16[16,4,16,128]{3,2,1,0:T(8,128)(2,1)S(1)} %pick_far.1), channel_id=1, replica_groups=mesh['y'=4,'w'=2,'x'=4,'p'=2,'q'=2,'r'=2,'c'=2] {'x','q','r'}, dimensions={0} | all-to-all | bytes 524288 | tf_op jit(solution)/shard_map/all_to_all | solution.py:275
  45.3 3.8 %collective-permute-start = (bf16[16,4,16,128]{3,2,1,0:T(8,128)(2,1)S(1)}, bf16[16,4,16,128]{3,2,1,0:T(8,128)(2,1)S(1)}, u32[]{:S(2)}, u32[]{:S(2)}) collective-permute-start(bf16[16,4,16,128]{3,2,1,0:T(8,128)(2,1)S(1)} %all_to_all.16.refs_1_), channel_id=1, source_target_pairs={{0,1},{1,0},{2,3},{3,2},{4,5},{5,4},{6,7},{7,6},{8,9},{9,8},{10,11... | collective-permute-start | bytes 786440 | tf_op jit(solution)/shard_map/ppermute | solution.py:276
  49.1 0.1 pad_add_fusion.place
  49.1 0.0 copy-done
  49.1 2.4 %correlate_near.1.near = bf16[4,2,208,128]{3,2,1,0:T(8,128)(2,1)S(1)} custom-call(s32[2]{0:T(128)S(1)} %pad_add_fusion.place, bf16[32,16,128]{2,1,0:T(8,128)(2,1)S(1)} %whiten.1.refs_0_, bf16[16,4,16,128]{3,2,1,0:T(8,128)(2,1)S(1)} %all_to_all.16.refs_1_, bf16[416,512]{1,0:T(8,128)(2,1)S(1)} %copy-done), custom_call_target="tpu_custom_call" | custom-call | tf_op jit(solution)/shard_map/correlate_near/pallas_call | solution.py:210
  51.5 0.0 collective-permute-done.refs_1_
  51.5 2.4 %correlate_far.1 = bf16[4,2,208,128]{3,2,1,0:T(8,128)(2,1)S(1)} custom-call(s32[2]{0:T(128)S(1)} %pad_add_fusion.place, bf16[4,2,208,128]{3,2,1,0:T(8,128)(2,1)S(1)} %correlate_near.1.near, bf16[32,16,128]{2,1,0:T(8,128)(2,1)S(1)} %whiten.1.refs_0_, bf16[16,4,16,128]{3,2,1,0:T(8,128)(2,1)S(1)} %collective-permute-done.refs_1_, bf16[416,512]{1,0:T(8,128)(2,1)S(1)} %copy-done), custom_call_target="tpu_custom_call" | custom-call | tf_op jit(solution)/shard_map/correlate_far/pallas_call | solution.py:210
  53.9 12.0 %all_to_all.17.parts = bf16[4,2,208,128]{3,2,1,0:T(8,128)(2,1)S(1)} all-to-all(bf16[4,2,208,128]{3,2,1,0:T(8,128)(2,1)S(1)} %correlate_far.1), channel_id=1, replica_groups=mesh['y'=4,'w'=2,'x'=4,'p'=2,'q'=2,'r'=2,'c'=2] {'y'}, dimensions={0} | all-to-all | bytes 851968 | tf_op jit(solution)/shard_map/all_to_all | solution.py:279
  65.9 0.6 fold.1
  66.5 12.5 %all-gather.1 = bf16[416,128]{1,0:T(8,128)(2,1)S(1)} all-gather(bf16[208,128]{1,0:T(8,128)(2,1)S(1)} %get-tuple-element.8), channel_id=3, replica_groups=mesh['y'=4,'w'=2,'x'=4,'p'=2,'q'=2,'r'=2,'c'=2] {'w'}, dimensions={0}, use_global_device_ids=true | all-gather | bytes 159744 | tf_op jit(solution)/shard_map/all_gather | solution.py:281
  78.9 0.7 finish.1
  79.7 0.7 reshape.7
Async XLA Ops:
  0.0 0.9 %copy-start.1 = (bf16[1,16,8,512]{3,2,1,0:T(8,128)(2,1)S(1)}, bf16[1,16,8,512]{3,2,1,0:T(8,128)(2,1)}, u32[]{:S(2)}) copy-start(bf16[1,16,8,512]{3,2,1,0:T(8,128)(2,1)} %param.5) | copy-start | bytes 393220
  0.9 0.7 copy-start.2
  2.9 18.5 %copy-start.3 = (s32[4]{0:T(128)S(1)}, s32[4]{0:T(128)}, u32[]{:S(2)}) copy-start(s32[4]{0:T(128)} %plan.3) | copy-start | bytes 52
  32.1 17.0 %copy-start = (bf16[416,512]{1,0:T(8,128)(2,1)S(1)}, bf16[416,512]{1,0:T(8,128)(2,1)}, u32[]{:S(2)}) copy-start(bf16[416,512]{1,0:T(8,128)(2,1)} %constant.10.clone.refs_2_) | copy-start | bytes 1277956
  45.3 6.2 %collective-permute-start = (bf16[16,4,16,128]{3,2,1,0:T(8,128)(2,1)S(1)}, bf16[16,4,16,128]{3,2,1,0:T(8,128)(2,1)S(1)}, u32[]{:S(2)}, u32[]{:S(2)}) collective-permute-start(bf16[16,4,16,128]{3,2,1,0:T(8,128)(2,1)S(1)} %all_to_all.16.refs_1_), channel_id=1, source_target_pairs={{0,1},{1,0},{2,3},{3,2},{4,5},{5,4},{6,7},{7,6},{8,9},{9,8},{10,11... | collective-permute-start | bytes 786440 | tf_op jit(solution)/shard_map/ppermute | solution.py:276

commit v3 on v2

--- a/solution.py
+++ b/solution.py
@@ -29,6 +29,7 @@
 F32 = jnp.float32
 BF16 = jnp.bfloat16
 VMEM_LIMIT = 16 * 1024 * 1024
+WHITEN_LIMIT = 60 * 1024 * 1024
 
 
 def angle_rows(times):
@@ -126,7 +127,7 @@
             pltpu.VMEM((SEGLEN, WIDE), F32),
             pltpu.SemaphoreType.DMA((2,)),
         ],
-        compiler_params=pltpu.CompilerParams(vmem_limit_bytes=VMEM_LIMIT),
+        compiler_params=pltpu.CompilerParams(vmem_limit_bytes=WHITEN_LIMIT),
         name="whiten",
     )(records, masks)
 
@@ -156,70 +157,57 @@
     )(plan, gathered)
 
 
-def correlate_half(core, white, source, table, lagged, own, wide, cross):
+def correlate_kernel(white, source, table, lagged, own, wide, cross):
     for tile in range(TILES):
         own[tile] = white[pl.ds(tile * 8, 8)].astype(F32).reshape(ROWS, LANES)
-        wide[tile] = source[pl.ds(tile * LINES, LINES)].astype(F32).reshape(LINES * STEPS * PIECE, LANES)
-
-    def pair(first, carry):
-        for part in range(2):
-            line = first * 2 + part
+        for core in range(2):
+            piece = source[core, pl.ds(tile * LINES, LINES)].astype(F32)
+            wide[tile, core] = piece.reshape(LINES * STEPS * PIECE, LANES)
+    for half in range(2):
+        own[TILES + half] = own[half] + own[half + 2]
+        wide[TILES + half] = wide[half] - wide[half + 2]
+
+    for line in range(LINES):
+        for core in range(2):
             for half in range(2):
                 right = []
                 for s in range(NSEG):
                     rows = pl.ds(line * (STEPS * PIECE) + s, SLOTS, stride=NSEG)
-                    right.append((wide[half, rows, :], wide[half + 2, rows, :]))
+                    right.append([wide[tile, core, rows, :] for tile in (half, half + 2, half + 4)])
                 for a in range(SB):
-                    real = imag = None
+                    sums = None
                     for s in range(NSEG):
                         row = pl.ds(a * NSEG + s, 1)
-                        left_re = jnp.broadcast_to(own[half, row, :], (SLOTS, LANES))
-                        left_im = jnp.broadcast_to(own[half + 2, row, :], (SLOTS, LANES))
-                        right_re, right_im = right[s]
-                        add_re = left_re * right_re + left_im * right_im
-                        add_im = left_im * right_re - left_re * right_im
-                        real = add_re if s == 0 else real + add_re
-                        imag = add_im if s == 0 else imag + add_im
-                    rows = pl.ds(part * ROWS + a * SLOTS, SLOTS)
-                    cross[rows, pl.ds(half * LANES, LANES)] = real
-                    cross[rows, pl.ds(FREQ + half * LANES, LANES)] = imag
-        high, low = split(cross[...])
+                        left = [own[tile, row, :] for tile in (half, half + 2, half + 4)]
+                        terms = [jnp.broadcast_to(x, (SLOTS, LANES)) * y for x, y in zip(left, right[s])]
+                        sums = terms if sums is None else [x + y for x, y in zip(sums, terms)]
+                    re_re, im_im, mixed = sums
+                    rows = pl.ds(core * ROWS + a * SLOTS, SLOTS)
+                    cross[line, rows, pl.ds(half * LANES, LANES)] = re_re + im_im
+                    cross[line, rows, pl.ds(FREQ + half * LANES, LANES)] = mixed + (im_im - re_re)
+        high, low = split(cross[line])
         both = mm_rows(table[...], high)
         out = (both[:KEPT] + (both[KEPT:] + mm_rows(table[pl.ds(0, KEPT), :], low))).astype(BF16)
-        for part in range(2):
-            lagged[first * 2 + part, core] = out[:, part * ROWS : (part + 1) * ROWS]
-        return carry
-
-    lax.fori_loop(0, LINES // 2, pair, 0)
-
-
-def correlate_near_kernel(place, *refs):
-    correlate_half(place[0], *refs)
-
-
-def correlate_far_kernel(place, near, *refs):
-    lagged = refs[3]
-    for line in range(LINES):
-        lagged[line, place[0]] = near[line, place[0]]
-    correlate_half(1 - place[0], *refs)
-
-
-def correlate(kernel, name, place, *arrays):
+        for core in range(2):
+            lagged[line, core] = out[:, core * ROWS : (core + 1) * ROWS]
+
+
+def correlate(*arrays):
     vmem = pl.BlockSpec(memory_space=pltpu.VMEM)
     arrays = arrays + (jnp.asarray(lag_tables()),)
     return pl.pallas_call(
-        kernel,
-        in_specs=[pl.BlockSpec(memory_space=pltpu.SMEM)] + [vmem] * len(arrays),
+        correlate_kernel,
+        in_specs=[vmem] * len(arrays),
         out_specs=vmem,
         out_shape=jax.ShapeDtypeStruct((LINES, 2, KEPT, ROWS), BF16),
         scratch_shapes=[
-            pltpu.VMEM((TILES, ROWS, LANES), F32),
-            pltpu.VMEM((TILES, LINES * STEPS * PIECE, LANES), F32),
-            pltpu.VMEM((2 * ROWS, WIDE), F32),
+            pltpu.VMEM((TILES + 2, ROWS, LANES), F32),
+            pltpu.VMEM((TILES + 2, 2, LINES * STEPS * PIECE, LANES), F32),
+            pltpu.VMEM((LINES, 2 * ROWS, WIDE), F32),
         ],
         compiler_params=pltpu.CompilerParams(vmem_limit_bytes=VMEM_LIMIT),
-        name=name,
-    )(place, *arrays)
+        name="correlate",
+    )(*arrays)
 
 
 def fold_kernel(place, parts, keep, send):
@@ -250,7 +238,7 @@
     column = lax.broadcasted_iota(jnp.int32, (ROWS, ROWS), 1)
     station, slot = (row // 2) % SB, (row // (2 * SB)) * 2 + row % 2
     order = jnp.where(column == station * SLOTS + slot, 1.0, 0.0).astype(BF16)
-    out[...] = mm_rows(order, total)[:, :LAGS].astype(BF16)
+    out[...] = mm_rows(order, total)[:, :LAGS].astype(BF16).reshape(STEPS, SB, 2, LAGS)
 
 
 def finish(place, keep, both):
@@ -259,7 +247,7 @@
         finish_kernel,
         in_specs=[pl.BlockSpec(memory_space=pltpu.SMEM), vmem, vmem],
         out_specs=vmem,
-        out_shape=jax.ShapeDtypeStruct((ROWS, LAGS), BF16),
+        out_shape=jax.ShapeDtypeStruct((STEPS, SB, 2, LAGS), BF16),
         compiler_params=pltpu.CompilerParams(vmem_limit_bytes=VMEM_LIMIT),
         name="finish",
     )(place, keep, both)
@@ -273,13 +261,12 @@
     ends = lax.all_gather(picked, "p", axis=0, tiled=False)
     spread = pick(pick_far_kernel, plan, ends, (SPREAD, STEPS, PIECE, LANES), "pick_far")
     near = lax.all_to_all(spread, ("x", "q", "r"), 0, 0, tiled=True)
-    far = lax.ppermute(near, "c", [(0, 1), (1, 0)])
-    lagged = correlate(correlate_near_kernel, "correlate_near", place, white, near)
-    lagged = correlate(correlate_far_kernel, "correlate_far", place, lagged, white, far)
+    source = lax.all_gather(near, "c", axis=0, tiled=False)
+    lagged = correlate(white, source)
     parts = lax.all_to_all(lagged, "y", 0, 0, tiled=True)
     keep, send = fold(place, parts)
     both = lax.all_gather(send, "w", axis=0, tiled=False)
-    return finish(place, keep, both).reshape(STEPS, SB, 2, LAGS)
+    return finish(place, keep, both)
 
 
 def solution(mesh):

time: 80.6 us -> 79 us (0.980)
  blocking collectives: 65.6 us -> 57.6 us
  waiting for transfers between devices: 0.01 us -> 7.77 us
  local copies, waits for them, and re-layouts: 2.28 us -> 0.01 us
    all_to_all x1 -> x0, blocking collectives: 12 us -> none  [shards(): parts = lax.all_to_all(lagged, 'y', 0, 0, tiled=True)]
    all_to_all x0 -> x1, waiting for transfers between devices: none -> 7.77 us  [shards(): parts = lax.all_to_all(lagged, 'y', 0, 0, tiled=True)]
    all_to_all x0 -> x1, starting transfers between devices: none -> 4.18 us  [shards(): parts = lax.all_to_all(lagged, 'y', 0, 0, tiled=True)]
    all_gather x0 -> x1, blocking collectives: none -> 3.78 us  [shards(): source = lax.all_gather(near, 'c', axis=0, tiled=False)]
    ppermute x1 -> x0, starting transfers between devices: 3.75 us -> none  [shards(): far = lax.ppermute(near, 'c', [(0, 1), (1, 0)])]
    unnamed x8 -> x6, local copies, waits for them, and re-layouts: 1.6 us -> 0.01 us
    pallas_call x2 -> x1, Pallas kernels: 4.73 us -> 3.48 us  [correlate(): pl.pallas_call(correlate_kernel, in_specs=[vmem] * len(arrays), out_specs...]
    pallas_call x1, Pallas kernels: 1.33 us -> 2.3 us  [whiten(): pl.pallas_call(whiten_kernel, in_specs=[hbm, hbm], out_specs=pl.BlockSpec...]
  transfers between devices with their start and end apart: 1 -> 1, of which waited for: 0 -> 1; matrix products, arithmetic and copies ran while one was open for 0% -> 0% of each run, Pallas kernels for 3% -> 0%
where the time goes in v3:
time: 79 us; the launch traced here: 78.6 us
  blocking collectives  57.6 us (73%)
  Pallas kernels  8.92 us (11%)
  waiting for transfers between devices  7.77 us (10%)
  starting transfers between devices  4.18 us (5%)
    all_to_all x1, blocking collectives, shards(): pieces = lax.all_to_all(white, ('x', 'q', 'r', 'c'), 0, 0, tiled=True)  19.2 us
    all_to_all x1, blocking collectives, shards(): near = lax.all_to_all(spread, ('x', 'q', 'r'), 0, 0, tiled=True)  12.6 us
    all_gather x1, blocking collectives, shards(): both = lax.all_gather(send, 'w', axis=0, tiled=False)  12.5 us
    all_gather x1, blocking collectives, shards(): ends = lax.all_gather(picked, 'p', axis=0, tiled=False)  9.57 us
    all_to_all x1, waiting for transfers between devices, shards(): parts = lax.all_to_all(lagged, 'y', 0, 0, tiled=True)  7.77 us
    all_to_all x1, starting transfers between devices, shards(): parts = lax.all_to_all(lagged, 'y', 0, 0, tiled=True)  4.18 us
    all_gather x1, blocking collectives, shards(): source = lax.all_gather(near, 'c', axis=0, tiled=False)  3.78 us
    pallas_call x1, Pallas kernels, correlate(): pl.pallas_call(correlate_kernel, in_specs=[vmem] * len(arrays), out_specs...  3.48 us
  transfers between devices with their start and end apart: 1, of which 1 were waited for; matrix products, arithmetic and copies ran while one was open for 0% of the time, Pallas kernels for 0%

profile of v3, /device:TPU:1, one launch (start us, length us, event | category | flops | bytes accessed | tf_op | source)
XLA Modules:
  0.0 78.6 jit_solution(10672848260442514439)
XLA Ops:
  0.0 2.3 %whiten.1.white = bf16[32,16,128]{2,1,0:T(8,128)(2,1)} custom-call(bf16[128,512]{1,0:T(8,128)(2,1)} %bitcast.12, s32[8,16]{1,0:T(8,128)} %bitcast.13), custom_call_target="tpu_custom_call" | custom-call | tf_op jit(solution)/shard_map/whiten/pallas_call | solution.py:119
  2.3 0.0 copy-start.2
  2.3 19.2 %all_to_all.15.gathered = bf16[32,16,128]{2,1,0:T(8,128)(2,1)S(1)} all-to-all(bf16[32,16,128]{2,1,0:T(8,128)(2,1)} %whiten.1.white), channel_id=1, replica_groups=mesh['y'=4,'w'=2,'x'=4,'p'=2,'q'=2,'r'=2,'c'=2] {'x','q','r','c'}, dimensions={0} | all-to-all | bytes 262144 | tf_op jit(solution)/shard_map/all_to_all | solution.py:259
  21.5 0.0 copy-done.2
  21.5 0.6 pick_near.1
  22.1 9.6 %all-gather = bf16[8,16,128]{2,1,0:T(8,128)(2,1)S(1)} all-gather(bf16[4,16,128]{2,1,0:T(8,128)(2,1)S(1)} %pick_near.1), channel_id=2, replica_groups=mesh['y'=4,'w'=2,'x'=4,'p'=2,'q'=2,'r'=2,'c'=2] {'p'}, dimensions={0}, use_global_device_ids=true | all-gather | bytes 49152 | tf_op jit(solution)/shard_map/all_gather | solution.py:261
  31.7 0.6 pick_far.1
  32.3 12.6 %all_to_all.16 = bf16[16,4,16,128]{3,2,1,0:T(8,128)(2,1)S(1)} all-to-all(bf16[16,4,16,128]{3,2,1,0:T(8,128)(2,1)S(1)} %pick_far.1), channel_id=1, replica_groups=mesh['y'=4,'w'=2,'x'=4,'p'=2,'q'=2,'r'=2,'c'=2] {'x','q','r'}, dimensions={0} | all-to-all | bytes 524288 | tf_op jit(solution)/shard_map/all_to_all | solution.py:263
  44.9 0.0 copy-start
  44.9 0.0 copy-start.1
  44.9 3.8 %all-gather.1 = bf16[32,4,16,128]{3,2,1,0:T(8,128)(2,1)S(1)} all-gather(bf16[16,4,16,128]{3,2,1,0:T(8,128)(2,1)S(1)} %all_to_all.16), channel_id=3, replica_groups=mesh['y'=4,'w'=2,'x'=4,'p'=2,'q'=2,'r'=2,'c'=2] {'c'}, dimensions={0}, use_global_device_ids=true | all-gather | bytes 786432 | tf_op jit(solution)/shard_map/all_gather | solution.py:264
  48.7 0.0 copy-done
  48.7 0.0 copy-done.1
  48.7 3.5 %correlate.1 = bf16[4,2,208,128]{3,2,1,0:T(8,128)(2,1)} custom-call(bf16[32,16,128]{2,1,0:T(8,128)(2,1)S(1)} %copy-done, bf16[2,16,4,16,128]{4,3,2,1,0:T(8,128)(2,1)S(1)} %bitcast.9, bf16[416,512]{1,0:T(8,128)(2,1)S(1)} %copy-done.1), custom_call_target="tpu_custom_call" | custom-call | tf_op jit(solution)/shard_map/correlate/pallas_call | solution.py:198
  52.2 4.2 %all-to-all-start.2 = ((bf16[4,2,208,128]{3,2,1,0:T(8,128)(2,1)}), bf16[4,2,208,128]{3,2,1,0:T(8,128)(2,1)S(1)}, u32[]{:S(2)}, u32[]{:S(2)}) async-start(bf16[4,2,208,128]{3,2,1,0:T(8,128)(2,1)} %correlate.1), calls=%async_computation.2 | async-start | bytes 851968 | tf_op jit(solution)/shard_map/all_to_all | solution.py:266
  56.3 0.1 pad_add_fusion.place
  56.4 7.8 %all-to-all-done.2.parts = bf16[4,2,208,128]{3,2,1,0:T(8,128)(2,1)S(1)} async-done(((bf16[4,2,208,128]{3,2,1,0:T(8,128)(2,1)}), bf16[4,2,208,128]{3,2,1,0:T(8,128)(2,1)S(1)}, u32[]{:S(2)}, u32[]{:S(2)}) %all-to-all-start.2) | async-done | bytes 426016 | tf_op jit(solution)/shard_map/all_to_all | solution.py:266
  64.2 0.6 fold.1
  64.8 12.5 %all-gather.2 = bf16[416,128]{1,0:T(8,128)(2,1)S(1)} all-gather(bf16[208,128]{1,0:T(8,128)(2,1)S(1)} %get-tuple-element.8), channel_id=4, replica_groups=mesh['y'=4,'w'=2,'x'=4,'p'=2,'q'=2,'r'=2,'c'=2] {'w'}, dimensions={0}, use_global_device_ids=true | all-gather | bytes 159744 | tf_op jit(solution)/shard_map/all_gather | solution.py:268
  77.3 1.4 %finish.1 = bf16[4,16,2,201]{3,2,1,0:T(2,128)(2,1)} custom-call(s32[2]{0:T(128)S(1)} %pad_add_fusion.place, f32[208,128]{1,0:T(8,128)S(1)} %get-tuple-element.7.keep, bf16[2,208,128]{2,1,0:T(8,128)(2,1)S(1)} %bitcast.10), custom_call_target="tpu_custom_call" | custom-call | tf_op jit(solution)/shard_map/finish/pallas_call | solution.py:246
Async XLA Ops:
  2.3 19.2 %copy-start.2 = (s32[4]{0:T(128)S(1)}, s32[4]{0:T(128)}, u32[]{:S(2)}) copy-start(s32[4]{0:T(128)} %plan.3) | copy-start | bytes 52
  44.9 3.8 %copy-start = (bf16[32,16,128]{2,1,0:T(8,128)(2,1)S(1)}, bf16[32,16,128]{2,1,0:T(8,128)(2,1)}, u32[]{:S(2)}) copy-start(bf16[32,16,128]{2,1,0:T(8,128)(2,1)} %whiten.1.white) | copy-start | bytes 393220
  44.9 3.8 %copy-start.1 = (bf16[416,512]{1,0:T(8,128)(2,1)S(1)}, bf16[416,512]{1,0:T(8,128)(2,1)}, u32[]{:S(2)}) copy-start(bf16[416,512]{1,0:T(8,128)(2,1)} %constant.10.clone.table) | copy-start | bytes 1277956
  52.2 12.0 %all-to-all-start.2 = ((bf16[4,2,208,128]{3,2,1,0:T(8,128)(2,1)}), bf16[4,2,208,128]{3,2,1,0:T(8,128)(2,1)S(1)}, u32[]{:S(2)}, u32[]{:S(2)}) async-start(bf16[4,2,208,128]{3,2,1,0:T(8,128)(2,1)} %correlate.1), calls=%async_computation.2 | async-start | bytes 851968 | tf_op jit(solution)/shard_map/all_to_all | solution.py:266

commit v4 on v3

--- a/solution.py
+++ b/solution.py
@@ -29,7 +29,6 @@
 F32 = jnp.float32
 BF16 = jnp.bfloat16
 VMEM_LIMIT = 16 * 1024 * 1024
-WHITEN_LIMIT = 60 * 1024 * 1024
 
 
 def angle_rows(times):
@@ -69,10 +68,15 @@
     return matrix, count.astype(F32)
 
 
-def whiten_kernel(records, mask, white, raw_buffer, mask_buffer, trig, sems):
+def unit_of(tile, pair):
+    return (pair // LINES) * (TILES * LINES) + tile * LINES + pair % LINES
+
+
+def whiten_kernel(records, mask, plan, white, steps, raw_buffer, mask_buffer, plan_buffer, trig, sems):
     fetches = [
         pltpu.make_async_copy(records, raw_buffer, sems.at[0]),
         pltpu.make_async_copy(mask, mask_buffer, sems.at[1]),
+        pltpu.make_async_copy(plan, plan_buffer, sems.at[2]),
     ]
     for fetch in fetches:
         fetch.start()
@@ -111,36 +115,49 @@
         lanes = slice((tile % 2) * LANES, (tile % 2 + 1) * LANES)
         part = (spec_part[:, lanes] * weight[:, lanes]).astype(BF16)
         for group in range(ROWS // PIECE):
-            white[tile * (ROWS // PIECE) + group] = part[group * PIECE : (group + 1) * PIECE]
-
-
-def whiten(records, masks):
+            white[unit_of(tile, group)] = part[group * PIECE : (group + 1) * PIECE]
+    for k in range(STEPS):
+        steps[k] = jnp.full((PIECE, LANES), plan_buffer[k], jnp.int32)
+
+
+def whiten(records, masks, plan):
     hbm = pl.BlockSpec(memory_space=pltpu.HBM)
+    vmem = pl.BlockSpec(memory_space=pltpu.VMEM)
     return pl.pallas_call(
         whiten_kernel,
-        in_specs=[hbm, hbm],
-        out_specs=pl.BlockSpec(memory_space=pltpu.VMEM),
-        out_shape=jax.ShapeDtypeStruct((UNITS, PIECE, LANES), BF16),
+        in_specs=[hbm] * 3,
+        out_specs=[vmem] * 2,
+        out_shape=[pltpu.VMEM((UNITS, PIECE, LANES), BF16), pltpu.VMEM((STEPS, PIECE, LANES), jnp.int32)],
         scratch_shapes=[
             pltpu.VMEM((ROWS, SEGLEN), BF16),
             pltpu.VMEM((NSEG, SB), jnp.int32),
+            pltpu.SMEM((STEPS,), jnp.int32),
             pltpu.VMEM((SEGLEN, WIDE), F32),
-            pltpu.SemaphoreType.DMA((2,)),
+            pltpu.SemaphoreType.DMA((3,)),
         ],
-        compiler_params=pltpu.CompilerParams(vmem_limit_bytes=WHITEN_LIMIT),
+        compiler_params=pltpu.CompilerParams(vmem_limit_bytes=VMEM_LIMIT),
         name="whiten",
-    )(records, masks)
-
-
-def pick_near_kernel(plan, gathered, picked):
+    )(*(pltpu.with_memory_space_constraint(x, pltpu.HBM) for x in (records, masks, plan)))
+
+
+def pick_near_kernel(steps, gathered, picked):
+    places = []
     for k in range(STEPS):
-        block = plan[k]
-        picked[k] = gathered[(block // 16) * 8 + block % 8]
-
-
-def pick_far_kernel(plan, gathered, spread):
+        block = steps[k]
+        q, x, rc = (block // 4) % 2, block // 16, block % 4
+        places.append(q * 16 + x * 4 + rc)
+    pieces = [jnp.zeros((PIECE, LANES), F32)] * STEPS
+    for unit in range(UNITS):
+        candidate = gathered[unit].astype(F32)
+        pieces = [jnp.where(place == unit, candidate, piece) for place, piece in zip(places, pieces)]
     for k in range(STEPS):
-        piece = gathered[(plan[k] // 8) % 2, k]
+        picked[k] = pieces[k].astype(BF16)
+
+
+def pick_far_kernel(steps, gathered, spread):
+    for k in range(STEPS):
+        first = (steps[k] // 8) % 2 == 0
+        piece = jnp.where(first, gathered[0, k].astype(F32), gathered[1, k].astype(F32)).astype(BF16)
         for to in range(SPREAD):
             spread[to, k] = piece
 
@@ -149,7 +166,7 @@
     vmem = pl.BlockSpec(memory_space=pltpu.VMEM)
     return pl.pallas_call(
         kernel,
-        in_specs=[pl.BlockSpec(memory_space=pltpu.SMEM), vmem],
+        in_specs=[vmem, vmem],
         out_specs=vmem,
         out_shape=jax.ShapeDtypeStruct(shape, BF16),
         compiler_params=pltpu.CompilerParams(vmem_limit_bytes=VMEM_LIMIT),
@@ -159,10 +176,13 @@
 
 def correlate_kernel(white, source, table, lagged, own, wide, cross):
     for tile in range(TILES):
-        own[tile] = white[pl.ds(tile * 8, 8)].astype(F32).reshape(ROWS, LANES)
-        for core in range(2):
-            piece = source[core, pl.ds(tile * LINES, LINES)].astype(F32)
-            wide[tile, core] = piece.reshape(LINES * STEPS * PIECE, LANES)
+        for q in range(2):
+            units = white[pl.ds(unit_of(tile, q * LINES), LINES)].astype(F32)
+            own[tile, pl.ds(q * (LINES * PIECE), LINES * PIECE), :] = units.reshape(LINES * PIECE, LANES)
+            for core in range(2):
+                piece = source[core, pl.ds(q * 8 + tile * 2, 2)].astype(F32)
+                rows = pl.ds(q * (2 * STEPS * PIECE), 2 * STEPS * PIECE)
+                wide[tile, core, rows, :] = piece.reshape(2 * STEPS * PIECE, LANES)
     for half in range(2):
         own[TILES + half] = own[half] + own[half + 2]
         wide[TILES + half] = wide[half] - wide[half + 2]
@@ -199,7 +219,7 @@
         correlate_kernel,
         in_specs=[vmem] * len(arrays),
         out_specs=vmem,
-        out_shape=jax.ShapeDtypeStruct((LINES, 2, KEPT, ROWS), BF16),
+        out_shape=pltpu.VMEM((LINES, 2, KEPT, ROWS), BF16),
         scratch_shapes=[
             pltpu.VMEM((TILES + 2, ROWS, LANES), F32),
             pltpu.VMEM((TILES + 2, 2, LINES * STEPS * PIECE, LANES), F32),
@@ -255,12 +275,12 @@
 
 def shards(records, masks, plan):
     place = jnp.stack([lax.axis_index("c"), lax.axis_index("w")]).astype(jnp.int32)
-    white = whiten(records.reshape(ROWS, SEGLEN), masks[0].T)
-    pieces = lax.all_to_all(white, ("x", "q", "r", "c"), 0, 0, tiled=True)
-    picked = pick(pick_near_kernel, plan, pieces, (STEPS, PIECE, LANES), "pick_near")
+    white, steps = whiten(records.reshape(ROWS, SEGLEN), masks[0].T, plan)
+    pieces = lax.all_to_all(white, ("q", "x", "r", "c"), 0, 0, tiled=True)
+    picked = pick(pick_near_kernel, steps, pieces, (STEPS, PIECE, LANES), "pick_near")
     ends = lax.all_gather(picked, "p", axis=0, tiled=False)
-    spread = pick(pick_far_kernel, plan, ends, (SPREAD, STEPS, PIECE, LANES), "pick_far")
-    near = lax.all_to_all(spread, ("x", "q", "r"), 0, 0, tiled=True)
+    spread = pick(pick_far_kernel, steps, ends, (SPREAD, STEPS, PIECE, LANES), "pick_far")
+    near = lax.all_to_all(spread, ("q", "x", "r"), 0, 0, tiled=True)
     source = lax.all_gather(near, "c", axis=0, tiled=False)
     lagged = correlate(white, source)
     parts = lax.all_to_all(lagged, "y", 0, 0, tiled=True)

time: 79 us -> 76.3 us (0.966)
  Pallas kernels: 8.92 us -> 7.32 us
  blocking collectives: 57.6 us -> 56.7 us
    pallas_call x3, Pallas kernels: 3.47 us -> 1.86 us  [the longest x1 1.68 us: whiten(): pl.pallas_call(whiten_kernel, in_specs=[hbm] * 3, out_specs=[vmem] * 2, o...]
where the time goes in v4:
time: 76.3 us; the launch traced here: 76.1 us
  blocking collectives  56.7 us (74%)
  waiting for transfers between devices  7.79 us (10%)
  Pallas kernels  7.32 us (10%)
  starting transfers between devices  4.18 us (5%)
    all_to_all x1, blocking collectives, shards(): pieces = lax.all_to_all(white, ('q', 'x', 'r', 'c'), 0, 0, tiled=True)  18.3 us
    all_to_all x1, blocking collectives, shards(): near = lax.all_to_all(spread, ('q', 'x', 'r'), 0, 0, tiled=True)  12.8 us
    all_gather x1, blocking collectives, shards(): both = lax.all_gather(send, 'w', axis=0, tiled=False)  12.6 us
    all_gather x1, blocking collectives, shards(): ends = lax.all_gather(picked, 'p', axis=0, tiled=False)  9.37 us
    all_to_all x1, waiting for transfers between devices, shards(): parts = lax.all_to_all(lagged, 'y', 0, 0, tiled=True)  7.79 us
    all_to_all x1, starting transfers between devices, shards(): parts = lax.all_to_all(lagged, 'y', 0, 0, tiled=True)  4.18 us
    all_gather x1, blocking collectives, shards(): source = lax.all_gather(near, 'c', axis=0, tiled=False)  3.59 us
    pallas_call x1, Pallas kernels, correlate(): pl.pallas_call(correlate_kernel, in_specs=[vmem] * len(arrays), out_specs...  3.49 us
  transfers between devices with their start and end apart: 1, of which 1 were waited for; matrix products, arithmetic and copies ran while one was open for 0% of the time, Pallas kernels for 0%

profile of v4, /device:TPU:1, one launch (start us, length us, event | category | flops | bytes accessed | tf_op | source)
XLA Modules:
  0.0 76.1 jit_solution(9431805526909031886)
XLA Ops:
  0.0 1.7 %whiten.1 = (bf16[32,16,128]{2,1,0:T(8,128)(2,1)S(1)}, s32[4,16,128]{2,1,0:T(8,128)S(1)}) custom-call(bf16[128,512]{1,0:T(8,128)(2,1)} %bitcast.12, s32[8,16]{1,0:T(8,128)} %bitcast.13, s32[4]{0:T(128)} %plan.1), custom_call_target="tpu_custom_call" | custom-call | tf_op jit(solution)/shard_map/whiten/pallas_call | solution.py:126
  1.7 18.3 %all_to_all.15.gathered = bf16[32,16,128]{2,1,0:T(8,128)(2,1)S(1)} all-to-all(bf16[32,16,128]{2,1,0:T(8,128)(2,1)S(1)} %get-tuple-element.9.white), channel_id=1, replica_groups=mesh['y'=4,'w'=2,'x'=4,'p'=2,'q'=2,'r'=2,'c'=2] {'q','x','r','c'}, dimensions={0} | all-to-all | bytes 262144 | tf_op jit(solution)/shard_map/all_to_all | solution.py:279
  20.0 0.1 pick_near.1
  20.1 9.4 %all-gather = bf16[8,16,128]{2,1,0:T(8,128)(2,1)S(1)} all-gather(bf16[4,16,128]{2,1,0:T(8,128)(2,1)S(1)} %pick_near.1), channel_id=2, replica_groups=mesh['y'=4,'w'=2,'x'=4,'p'=2,'q'=2,'r'=2,'c'=2] {'p'}, dimensions={0}, use_global_device_ids=true | all-gather | bytes 49152 | tf_op jit(solution)/shard_map/all_gather | solution.py:281
  29.6 12.8 %all_to_all.16 = bf16[16,4,16,128]{3,2,1,0:T(8,128)(2,1)S(1)} all-to-all(bf16[16,4,16,128]{3,2,1,0:T(8,128)(2,1)S(1)} %pick_far.1), channel_id=1, replica_groups=mesh['y'=4,'w'=2,'x'=4,'p'=2,'q'=2,'r'=2,'c'=2] {'q','x','r'}, dimensions={0} | all-to-all | bytes 524288 | tf_op jit(solution)/shard_map/all_to_all | solution.py:283
  42.3 0.0 copy-start
  42.3 3.6 %all-gather.1 = bf16[32,4,16,128]{3,2,1,0:T(8,128)(2,1)S(1)} all-gather(bf16[16,4,16,128]{3,2,1,0:T(8,128)(2,1)S(1)} %all_to_all.16), channel_id=3, replica_groups=mesh['y'=4,'w'=2,'x'=4,'p'=2,'q'=2,'r'=2,'c'=2] {'c'}, dimensions={0}, use_global_device_ids=true | all-gather | bytes 786432 | tf_op jit(solution)/shard_map/all_gather | solution.py:284
  45.9 0.0 copy-done
  45.9 3.5 %correlate.1 = bf16[4,2,208,128]{3,2,1,0:T(8,128)(2,1)} custom-call(bf16[32,16,128]{2,1,0:T(8,128)(2,1)S(1)} %get-tuple-element.9.white, bf16[2,16,4,16,128]{4,3,2,1,0:T(8,128)(2,1)S(1)} %bitcast.9, bf16[416,512]{1,0:T(8,128)(2,1)S(1)} %copy-done), custom_call_target="tpu_custom_call" | custom-call | tf_op jit(solution)/shard_map/correlate/pallas_call | solution.py:218
  49.4 4.2 %all-to-all-start.2 = ((bf16[4,2,208,128]{3,2,1,0:T(8,128)(2,1)}), bf16[4,2,208,128]{3,2,1,0:T(8,128)(2,1)S(1)}, u32[]{:S(2)}, u32[]{:S(2)}) async-start(bf16[4,2,208,128]{3,2,1,0:T(8,128)(2,1)} %correlate.1), calls=%async_computation.2 | async-start | bytes 851968 | tf_op jit(solution)/shard_map/all_to_all | solution.py:286
  53.6 0.1 pad_add_fusion.place
  53.7 7.8 %all-to-all-done.2.parts = bf16[4,2,208,128]{3,2,1,0:T(8,128)(2,1)S(1)} async-done(((bf16[4,2,208,128]{3,2,1,0:T(8,128)(2,1)}), bf16[4,2,208,128]{3,2,1,0:T(8,128)(2,1)S(1)}, u32[]{:S(2)}, u32[]{:S(2)}) %all-to-all-start.2) | async-done | bytes 426016 | tf_op jit(solution)/shard_map/all_to_all | solution.py:286
  61.5 0.6 fold.1
  62.1 12.6 %all-gather.2 = bf16[416,128]{1,0:T(8,128)(2,1)S(1)} all-gather(bf16[208,128]{1,0:T(8,128)(2,1)S(1)} %get-tuple-element.12), channel_id=4, replica_groups=mesh['y'=4,'w'=2,'x'=4,'p'=2,'q'=2,'r'=2,'c'=2] {'w'}, dimensions={0}, use_global_device_ids=true | all-gather | bytes 159744 | tf_op jit(solution)/shard_map/all_gather | solution.py:288
  74.7 1.4 %finish.1 = bf16[4,16,2,201]{3,2,1,0:T(2,128)(2,1)} custom-call(s32[2]{0:T(128)S(1)} %pad_add_fusion.place, f32[208,128]{1,0:T(8,128)S(1)} %get-tuple-element.11.keep, bf16[2,208,128]{2,1,0:T(8,128)(2,1)S(1)} %bitcast.10), custom_call_target="tpu_custom_call" | custom-call | tf_op jit(solution)/shard_map/finish/pallas_call | solution.py:266
  (1 shorter events, 0.0 us)
Async XLA Ops:
  42.3 3.6 %copy-start = (bf16[416,512]{1,0:T(8,128)(2,1)S(1)}, bf16[416,512]{1,0:T(8,128)(2,1)}, u32[]{:S(2)}) copy-start(bf16[416,512]{1,0:T(8,128)(2,1)} %constant.10.clone.table) | copy-start | bytes 1277956
  49.4 12.0 %all-to-all-start.2 = ((bf16[4,2,208,128]{3,2,1,0:T(8,128)(2,1)}), bf16[4,2,208,128]{3,2,1,0:T(8,128)(2,1)S(1)}, u32[]{:S(2)}, u32[]{:S(2)}) async-start(bf16[4,2,208,128]{3,2,1,0:T(8,128)(2,1)} %correlate.1), calls=%async_computation.2 | async-start | bytes 851968 | tf_op jit(solution)/shard_map/all_to_all | solution.py:286

commit v5 on v4

--- a/solution.py
+++ b/solution.py
@@ -230,8 +230,9 @@
     )(*arrays)
 
 
-def fold_kernel(place, parts, keep, send):
-    mine, other = place[1], 1 - place[1]
+def fold_kernel(parts, keep, send):
+    mine = lax.axis_index("w")
+    other = 1 - mine
     keep_sum, send_sum = parts[0, mine].astype(F32), parts[0, other].astype(F32)
     for quad in range(1, LINES):
         keep_sum = keep_sum + parts[quad, mine].astype(F32)
@@ -240,20 +241,20 @@
     send[...] = send_sum.astype(BF16)
 
 
-def fold(place, parts):
+def fold(parts):
     vmem = pl.BlockSpec(memory_space=pltpu.VMEM)
     return pl.pallas_call(
         fold_kernel,
-        in_specs=[pl.BlockSpec(memory_space=pltpu.SMEM), vmem],
+        in_specs=[vmem],
         out_specs=[vmem, vmem],
         out_shape=[jax.ShapeDtypeStruct((KEPT, ROWS), F32), jax.ShapeDtypeStruct((KEPT, ROWS), BF16)],
         compiler_params=pltpu.CompilerParams(vmem_limit_bytes=VMEM_LIMIT),
         name="fold",
-    )(place, parts)
-
-
-def finish_kernel(place, keep, both, out):
-    total = (keep[...] + both[1 - place[1]].astype(F32)).astype(BF16)
+    )(parts)
+
+
+def finish_kernel(keep, both, out):
+    total = (keep[...] + both[1 - lax.axis_index("w")].astype(F32)).astype(BF16)
     row = lax.broadcasted_iota(jnp.int32, (ROWS, ROWS), 0)
     column = lax.broadcasted_iota(jnp.int32, (ROWS, ROWS), 1)
     station, slot = (row // 2) % SB, (row // (2 * SB)) * 2 + row % 2
@@ -261,20 +262,19 @@
     out[...] = mm_rows(order, total)[:, :LAGS].astype(BF16).reshape(STEPS, SB, 2, LAGS)
 
 
-def finish(place, keep, both):
+def finish(keep, both):
     vmem = pl.BlockSpec(memory_space=pltpu.VMEM)
     return pl.pallas_call(
         finish_kernel,
-        in_specs=[pl.BlockSpec(memory_space=pltpu.SMEM), vmem, vmem],
+        in_specs=[vmem, vmem],
         out_specs=vmem,
         out_shape=jax.ShapeDtypeStruct((STEPS, SB, 2, LAGS), BF16),
         compiler_params=pltpu.CompilerParams(vmem_limit_bytes=VMEM_LIMIT),
         name="finish",
-    )(place, keep, both)
+    )(keep, both)
 
 
 def shards(records, masks, plan):
-    place = jnp.stack([lax.axis_index("c"), lax.axis_index("w")]).astype(jnp.int32)
     white, steps = whiten(records.reshape(ROWS, SEGLEN), masks[0].T, plan)
     pieces = lax.all_to_all(white, ("q", "x", "r", "c"), 0, 0, tiled=True)
     picked = pick(pick_near_kernel, steps, pieces, (STEPS, PIECE, LANES), "pick_near")
@@ -284,9 +284,9 @@
     source = lax.all_gather(near, "c", axis=0, tiled=False)
     lagged = correlate(white, source)
     parts = lax.all_to_all(lagged, "y", 0, 0, tiled=True)
-    keep, send = fold(place, parts)
+    keep, send = fold(parts)
     both = lax.all_gather(send, "w", axis=0, tiled=False)
-    return finish(place, keep, both)
+    return finish(keep, both)
 
 
 def solution(mesh):

time: 76.3 us -> 74.2 us (0.972)
  blocking collectives: 56.7 us -> 68.5 us
  waiting for transfers between devices: 7.79 us -> 0 us
  starting transfers between devices: 4.18 us -> 0 us
  Pallas kernels: 7.32 us -> 5.46 us
    all_to_all x0 -> x1, blocking collectives: none -> 11.8 us  [shards(): parts = lax.all_to_all(lagged, 'y', 0, 0, tiled=True)]
    all_to_all x1 -> x0, waiting for transfers between devices: 7.79 us -> none  [shards(): parts = lax.all_to_all(lagged, 'y', 0, 0, tiled=True)]
    all_to_all x1 -> x0, starting transfers between devices: 4.18 us -> none  [shards(): parts = lax.all_to_all(lagged, 'y', 0, 0, tiled=True)]
    pallas_call x2, Pallas kernels: 1.97 us -> 0.89 us  [the longest x1 0.83 us: finish(): pl.pallas_call(finish_kernel, in_specs=[vmem, vmem], out_specs=vmem, out_...]
    pallas_call x1, Pallas kernels: 3.49 us -> 2.71 us  [correlate(): pl.pallas_call(correlate_kernel, in_specs=[vmem] * len(arrays), out_specs...]
  transfers between devices with their start and end apart: 1 -> 0, of which waited for: 1 -> 0; matrix products, arithmetic and copies ran while one was open for 0% -> 0% of each run, Pallas kernels for 0% -> 0%
where the time goes in v5:
time: 74.2 us; the launch traced here: 74 us
  blocking collectives  68.5 us (92%)
  Pallas kernels  5.46 us (7%)
    all_to_all x1, blocking collectives, shards(): pieces = lax.all_to_all(white, ('q', 'x', 'r', 'c'), 0, 0, tiled=True)  18.3 us
    all_to_all x1, blocking collectives, shards(): near = lax.all_to_all(spread, ('q', 'x', 'r'), 0, 0, tiled=True)  12.8 us
    all_gather x1, blocking collectives, shards(): both = lax.all_gather(send, 'w', axis=0, tiled=False)  12.6 us
    all_to_all x1, blocking collectives, shards(): parts = lax.all_to_all(lagged, 'y', 0, 0, tiled=True)  11.8 us
    all_gather x1, blocking collectives, shards(): ends = lax.all_gather(picked, 'p', axis=0, tiled=False)  9.37 us
    all_gather x1, blocking collectives, shards(): source = lax.all_gather(near, 'c', axis=0, tiled=False)  3.59 us
    pallas_call x1, Pallas kernels, correlate(): pl.pallas_call(correlate_kernel, in_specs=[vmem] * len(arrays), out_specs...  2.71 us
    pallas_call x1, Pallas kernels, whiten(): pl.pallas_call(whiten_kernel, in_specs=[hbm] * 3, out_specs=[vmem] * 2, o...  1.68 us

profile of v5, /device:TPU:1, one launch (start us, length us, event | category | flops | bytes accessed | tf_op | source)
XLA Modules:
  0.0 74.0 jit_solution(9883327353945928888)
XLA Ops:
  0.0 1.7 %whiten.1 = (bf16[32,16,128]{2,1,0:T(8,128)(2,1)S(1)}, s32[4,16,128]{2,1,0:T(8,128)S(1)}) custom-call(bf16[128,512]{1,0:T(8,128)(2,1)} %bitcast.10, s32[8,16]{1,0:T(8,128)} %bitcast.11, s32[4]{0:T(128)} %plan.1), custom_call_target="tpu_custom_call" | custom-call | tf_op jit(solution)/shard_map/whiten/pallas_call | solution.py:126
  1.7 18.3 %all_to_all.15.gathered = bf16[32,16,128]{2,1,0:T(8,128)(2,1)S(1)} all-to-all(bf16[32,16,128]{2,1,0:T(8,128)(2,1)S(1)} %get-tuple-element.9.white), channel_id=1, replica_groups=mesh['y'=4,'w'=2,'x'=4,'p'=2,'q'=2,'r'=2,'c'=2] {'q','x','r','c'}, dimensions={0} | all-to-all | bytes 262144 | tf_op jit(solution)/shard_map/all_to_all | solution.py:279
  20.0 0.1 pick_near.1
  20.1 9.4 %all-gather = bf16[8,16,128]{2,1,0:T(8,128)(2,1)S(1)} all-gather(bf16[4,16,128]{2,1,0:T(8,128)(2,1)S(1)} %pick_near.1), channel_id=2, replica_groups=mesh['y'=4,'w'=2,'x'=4,'p'=2,'q'=2,'r'=2,'c'=2] {'p'}, dimensions={0}, use_global_device_ids=true | all-gather | bytes 49152 | tf_op jit(solution)/shard_map/all_gather | solution.py:281
  29.6 12.8 %all_to_all.16 = bf16[16,4,16,128]{3,2,1,0:T(8,128)(2,1)S(1)} all-to-all(bf16[16,4,16,128]{3,2,1,0:T(8,128)(2,1)S(1)} %pick_far.1), channel_id=1, replica_groups=mesh['y'=4,'w'=2,'x'=4,'p'=2,'q'=2,'r'=2,'c'=2] {'q','x','r'}, dimensions={0} | all-to-all | bytes 524288 | tf_op jit(solution)/shard_map/all_to_all | solution.py:283
  42.3 0.0 copy-start
  42.3 3.6 %all-gather.1 = bf16[32,4,16,128]{3,2,1,0:T(8,128)(2,1)S(1)} all-gather(bf16[16,4,16,128]{3,2,1,0:T(8,128)(2,1)S(1)} %all_to_all.16), channel_id=3, replica_groups=mesh['y'=4,'w'=2,'x'=4,'p'=2,'q'=2,'r'=2,'c'=2] {'c'}, dimensions={0}, use_global_device_ids=true | all-gather | bytes 786432 | tf_op jit(solution)/shard_map/all_gather | solution.py:284
  45.9 0.0 copy-done
  45.9 2.7 %correlate.1 = bf16[4,2,208,128]{3,2,1,0:T(8,128)(2,1)S(1)} custom-call(bf16[32,16,128]{2,1,0:T(8,128)(2,1)S(1)} %get-tuple-element.9.white, bf16[2,16,4,16,128]{4,3,2,1,0:T(8,128)(2,1)S(1)} %bitcast.7, bf16[416,512]{1,0:T(8,128)(2,1)S(1)} %copy-done), custom_call_target="tpu_custom_call" | custom-call | tf_op jit(solution)/shard_map/correlate/pallas_call | solution.py:218
  48.6 11.8 %all_to_all.17.parts = bf16[4,2,208,128]{3,2,1,0:T(8,128)(2,1)S(1)} all-to-all(bf16[4,2,208,128]{3,2,1,0:T(8,128)(2,1)S(1)} %correlate.1), channel_id=1, replica_groups=mesh['y'=4,'w'=2,'x'=4,'p'=2,'q'=2,'r'=2,'c'=2] {'y'}, dimensions={0} | all-to-all | bytes 851968 | tf_op jit(solution)/shard_map/all_to_all | solution.py:286
  60.5 0.1 fold.1
  60.5 12.6 %all-gather.2 = bf16[416,128]{1,0:T(8,128)(2,1)S(1)} all-gather(bf16[208,128]{1,0:T(8,128)(2,1)S(1)} %get-tuple-element.12), channel_id=4, replica_groups=mesh['y'=4,'w'=2,'x'=4,'p'=2,'q'=2,'r'=2,'c'=2] {'w'}, dimensions={0}, use_global_device_ids=true | all-gather | bytes 159744 | tf_op jit(solution)/shard_map/all_gather | solution.py:288
  73.2 0.8 %finish.1 = bf16[4,16,2,201]{3,2,1,0:T(2,128)(2,1)} custom-call(f32[208,128]{1,0:T(8,128)S(1)} %get-tuple-element.11.keep, bf16[2,208,128]{2,1,0:T(8,128)(2,1)S(1)} %bitcast.8), custom_call_target="tpu_custom_call" | custom-call | tf_op jit(solution)/shard_map/finish/pallas_call | solution.py:267
  (1 shorter events, 0.0 us)
Async XLA Ops:
  42.3 3.6 %copy-start = (bf16[416,512]{1,0:T(8,128)(2,1)S(1)}, bf16[416,512]{1,0:T(8,128)(2,1)}, u32[]{:S(2)}) copy-start(bf16[416,512]{1,0:T(8,128)(2,1)} %constant.2.clone.table) | copy-start | bytes 1277956

commit v6 on v5

--- a/solution.py
+++ b/solution.py
@@ -25,6 +25,8 @@
 SPREAD = 16
 SLOTS = 2 * STEPS
 KEPT = 208
+LAST = KEPT - SLOTS
+NEAR = LAGS // 2 - SLOTS // 2
 
 F32 = jnp.float32
 BF16 = jnp.bfloat16
@@ -41,7 +43,7 @@
     shifts = np.arange(LAGS) - LAGS // 2
     angles = 2.0 * math.pi * ((shifts[:, None] * np.arange(FREQ)[None, :]) % SEGLEN) / SEGLEN
     table = np.concatenate([np.cos(angles), -np.sin(angles)], axis=1) / math.sqrt(NSEG * FREQ * HOURS)
-    table = np.pad(table, ((0, KEPT - LAGS), (0, 0)))
+    table = np.concatenate([table, table[NEAR + 1 : NEAR + SLOTS]], axis=0)
     high = table.astype(BF16)
     return np.concatenate([high, (table - high.astype(np.float64)).astype(BF16)], axis=0)
 
@@ -52,6 +54,22 @@
 
 def mm_rows(left, right):
     return lax.dot_general(left, right, (((1,), (1,)), ((), ())), preferred_element_type=F32)
+
+
+def spare():
+    return lax.broadcasted_iota(jnp.int32, (SLOTS, ROWS), 0) > 0
+
+
+def pack(value, near):
+    high = value.astype(BF16)
+    rest = near - near.astype(BF16).astype(F32)
+    last = jnp.where(spare(), rest, value[LAST:])
+    return jnp.concatenate([high[: LAST - SLOTS], jnp.concatenate([value[LAST - SLOTS : LAST], last], axis=0).astype(BF16)], axis=0)
+
+
+def unpack(value):
+    near = value[NEAR : NEAR + SLOTS] + jnp.where(spare(), value[LAST:], 0.0)
+    return jnp.concatenate([value[:NEAR], near, value[NEAR + SLOTS :]], axis=0)
 
 
 def split(value):
@@ -207,9 +225,10 @@
                     cross[line, rows, pl.ds(FREQ + half * LANES, LANES)] = mixed + (im_im - re_re)
         high, low = split(cross[line])
         both = mm_rows(table[...], high)
-        out = (both[:KEPT] + (both[KEPT:] + mm_rows(table[pl.ds(0, KEPT), :], low))).astype(BF16)
+        out = both[:KEPT] + (both[KEPT:] + mm_rows(table[pl.ds(0, KEPT), :], low))
         for core in range(2):
-            lagged[line, core] = out[:, core * ROWS : (core + 1) * ROWS]
+            part = out[:, core * ROWS : (core + 1) * ROWS]
+            lagged[line, core] = pack(part, part[LAST:])
 
 
 def correlate(*arrays):
@@ -237,8 +256,9 @@
     for quad in range(1, LINES):
         keep_sum = keep_sum + parts[quad, mine].astype(F32)
         send_sum = send_sum + parts[quad, other].astype(F32)
-    keep[...] = keep_sum
-    send[...] = send_sum.astype(BF16)
+    keep[...] = unpack(keep_sum)
+    send_sum = unpack(send_sum)
+    send[...] = pack(send_sum, send_sum[NEAR : NEAR + SLOTS])
 
 
 def fold(parts):
@@ -254,7 +274,7 @@
 
 
 def finish_kernel(keep, both, out):
-    total = (keep[...] + both[1 - lax.axis_index("w")].astype(F32)).astype(BF16)
+    total = (keep[...] + unpack(both[1 - lax.axis_index("w")].astype(F32))).astype(BF16)
     row = lax.broadcasted_iota(jnp.int32, (ROWS, ROWS), 0)
     column = lax.broadcasted_iota(jnp.int32, (ROWS, ROWS), 1)
     station, slot = (row // 2) % SB, (row // (2 * SB)) * 2 + row % 2

time: 74.2 us -> 74.3 us (level)
  no operation moved by 1% of the time
where the time goes in v6:
time: 74.3 us; the launch traced here: 74 us
  blocking collectives  68.5 us (92%)
  Pallas kernels  5.46 us (7%)
    all_to_all x1, blocking collectives, shards(): pieces = lax.all_to_all(white, ('q', 'x', 'r', 'c'), 0, 0, tiled=True)  18.3 us
    all_to_all x1, blocking collectives, shards(): near = lax.all_to_all(spread, ('q', 'x', 'r'), 0, 0, tiled=True)  12.8 us
    all_gather x1, blocking collectives, shards(): both = lax.all_gather(send, 'w', axis=0, tiled=False)  12.6 us
    all_to_all x1, blocking collectives, shards(): parts = lax.all_to_all(lagged, 'y', 0, 0, tiled=True)  11.8 us
    all_gather x1, blocking collectives, shards(): ends = lax.all_gather(picked, 'p', axis=0, tiled=False)  9.37 us
    all_gather x1, blocking collectives, shards(): source = lax.all_gather(near, 'c', axis=0, tiled=False)  3.59 us
    pallas_call x1, Pallas kernels, correlate(): pl.pallas_call(correlate_kernel, in_specs=[vmem] * len(arrays), out_specs...  2.71 us
    pallas_call x1, Pallas kernels, whiten(): pl.pallas_call(whiten_kernel, in_specs=[hbm] * 3, out_specs=[vmem] * 2, o...  1.68 us

profile of v6, /device:TPU:1, one launch (start us, length us, event | category | flops | bytes accessed | tf_op | source)
XLA Modules:
  0.0 74.0 jit_solution(9246682377129333214)
XLA Ops:
  0.0 1.7 %whiten.1 = (bf16[32,16,128]{2,1,0:T(8,128)(2,1)S(1)}, s32[4,16,128]{2,1,0:T(8,128)S(1)}) custom-call(bf16[128,512]{1,0:T(8,128)(2,1)} %bitcast.10, s32[8,16]{1,0:T(8,128)} %bitcast.11, s32[4]{0:T(128)} %plan.1), custom_call_target="tpu_custom_call" | custom-call | tf_op jit(solution)/shard_map/whiten/pallas_call | solution.py:144
  1.7 18.3 %all_to_all.15.gathered = bf16[32,16,128]{2,1,0:T(8,128)(2,1)S(1)} all-to-all(bf16[32,16,128]{2,1,0:T(8,128)(2,1)S(1)} %get-tuple-element.9.white), channel_id=1, replica_groups=mesh['y'=4,'w'=2,'x'=4,'p'=2,'q'=2,'r'=2,'c'=2] {'q','x','r','c'}, dimensions={0} | all-to-all | bytes 262144 | tf_op jit(solution)/shard_map/all_to_all | solution.py:299
  20.0 0.1 pick_near.1
  20.1 9.4 %all-gather = bf16[8,16,128]{2,1,0:T(8,128)(2,1)S(1)} all-gather(bf16[4,16,128]{2,1,0:T(8,128)(2,1)S(1)} %pick_near.1), channel_id=2, replica_groups=mesh['y'=4,'w'=2,'x'=4,'p'=2,'q'=2,'r'=2,'c'=2] {'p'}, dimensions={0}, use_global_device_ids=true | all-gather | bytes 49152 | tf_op jit(solution)/shard_map/all_gather | solution.py:301
  29.6 12.8 %all_to_all.16 = bf16[16,4,16,128]{3,2,1,0:T(8,128)(2,1)S(1)} all-to-all(bf16[16,4,16,128]{3,2,1,0:T(8,128)(2,1)S(1)} %pick_far.1), channel_id=1, replica_groups=mesh['y'=4,'w'=2,'x'=4,'p'=2,'q'=2,'r'=2,'c'=2] {'q','x','r'}, dimensions={0} | all-to-all | bytes 524288 | tf_op jit(solution)/shard_map/all_to_all | solution.py:303
  42.3 0.0 copy-start
  42.3 3.6 %all-gather.1 = bf16[32,4,16,128]{3,2,1,0:T(8,128)(2,1)S(1)} all-gather(bf16[16,4,16,128]{3,2,1,0:T(8,128)(2,1)S(1)} %all_to_all.16), channel_id=3, replica_groups=mesh['y'=4,'w'=2,'x'=4,'p'=2,'q'=2,'r'=2,'c'=2] {'c'}, dimensions={0}, use_global_device_ids=true | all-gather | bytes 786432 | tf_op jit(solution)/shard_map/all_gather | solution.py:304
  45.9 0.0 copy-done
  45.9 2.7 %correlate.1 = bf16[4,2,208,128]{3,2,1,0:T(8,128)(2,1)S(1)} custom-call(bf16[32,16,128]{2,1,0:T(8,128)(2,1)S(1)} %get-tuple-element.9.white, bf16[2,16,4,16,128]{4,3,2,1,0:T(8,128)(2,1)S(1)} %bitcast.7, bf16[416,512]{1,0:T(8,128)(2,1)S(1)} %copy-done), custom_call_target="tpu_custom_call" | custom-call | tf_op jit(solution)/shard_map/correlate/pallas_call | solution.py:237
  48.6 11.8 %all_to_all.17.parts = bf16[4,2,208,128]{3,2,1,0:T(8,128)(2,1)S(1)} all-to-all(bf16[4,2,208,128]{3,2,1,0:T(8,128)(2,1)S(1)} %correlate.1), channel_id=1, replica_groups=mesh['y'=4,'w'=2,'x'=4,'p'=2,'q'=2,'r'=2,'c'=2] {'y'}, dimensions={0} | all-to-all | bytes 851968 | tf_op jit(solution)/shard_map/all_to_all | solution.py:306
  60.5 0.1 fold.1
  60.6 12.6 %all-gather.2 = bf16[416,128]{1,0:T(8,128)(2,1)S(1)} all-gather(bf16[208,128]{1,0:T(8,128)(2,1)S(1)} %get-tuple-element.12), channel_id=4, replica_groups=mesh['y'=4,'w'=2,'x'=4,'p'=2,'q'=2,'r'=2,'c'=2] {'w'}, dimensions={0}, use_global_device_ids=true | all-gather | bytes 159744 | tf_op jit(solution)/shard_map/all_gather | solution.py:308
  73.2 0.8 %finish.1 = bf16[4,16,2,201]{3,2,1,0:T(2,128)(2,1)} custom-call(f32[208,128]{1,0:T(8,128)S(1)} %get-tuple-element.11.keep, bf16[2,208,128]{2,1,0:T(8,128)(2,1)S(1)} %bitcast.8), custom_call_target="tpu_custom_call" | custom-call | tf_op jit(solution)/shard_map/finish/pallas_call | solution.py:287
  (1 shorter events, 0.0 us)
Async XLA Ops:
  42.3 3.6 %copy-start = (bf16[416,512]{1,0:T(8,128)(2,1)S(1)}, bf16[416,512]{1,0:T(8,128)(2,1)}, u32[]{:S(2)}) copy-start(bf16[416,512]{1,0:T(8,128)(2,1)} %constant.2.clone.table) | copy-start | bytes 1277956

commit v7 on v6

--- a/solution.py
+++ b/solution.py
@@ -173,11 +173,19 @@
 
 
 def pick_far_kernel(steps, gathered, spread):
+    pieces = []
     for k in range(STEPS):
         first = (steps[k] // 8) % 2 == 0
-        piece = jnp.where(first, gathered[0, k].astype(F32), gathered[1, k].astype(F32)).astype(BF16)
+        pieces.append(jnp.where(first, gathered[0, k].astype(F32), gathered[1, k].astype(F32)))
+    count = STEPS * PIECE
+    row = lax.broadcasted_iota(jnp.int32, (count, count), 0)
+    column = lax.broadcasted_iota(jnp.int32, (count, count), 1)
+    order = jnp.where(column == (row % SLOTS) * NSEG + row // SLOTS, 1.0, 0.0).astype(BF16)
+    ordered = mm(order, jnp.concatenate(pieces, axis=0).astype(BF16)).astype(BF16)
+    for part in range(STEPS):
+        piece = ordered[part * PIECE : (part + 1) * PIECE]
         for to in range(SPREAD):
-            spread[to, k] = piece
+            spread[to, part] = piece
 
 
 def pick(kernel, plan, gathered, shape, name):
@@ -192,26 +200,24 @@
     )(plan, gathered)
 
 
-def correlate_kernel(white, source, table, lagged, own, wide, cross):
+def correlate_kernel(white, source, table, lagged, own, cross):
     for tile in range(TILES):
         for q in range(2):
             units = white[pl.ds(unit_of(tile, q * LINES), LINES)].astype(F32)
             own[tile, pl.ds(q * (LINES * PIECE), LINES * PIECE), :] = units.reshape(LINES * PIECE, LANES)
-            for core in range(2):
-                piece = source[core, pl.ds(q * 8 + tile * 2, 2)].astype(F32)
-                rows = pl.ds(q * (2 * STEPS * PIECE), 2 * STEPS * PIECE)
-                wide[tile, core, rows, :] = piece.reshape(2 * STEPS * PIECE, LANES)
     for half in range(2):
         own[TILES + half] = own[half] + own[half + 2]
-        wide[TILES + half] = wide[half] - wide[half + 2]
 
     for line in range(LINES):
+        place = (line // 2) * 8 + line % 2
         for core in range(2):
             for half in range(2):
                 right = []
-                for s in range(NSEG):
-                    rows = pl.ds(line * (STEPS * PIECE) + s, SLOTS, stride=NSEG)
-                    right.append([wide[tile, core, rows, :] for tile in (half, half + 2, half + 4)])
+                for part in range(STEPS):
+                    both = [source[core, place + tile * 2, part].astype(F32) for tile in (half, half + 2)]
+                    for s in range(2):
+                        re, im = [x[s * SLOTS : (s + 1) * SLOTS] for x in both]
+                        right.append([re, im, re - im])
                 for a in range(SB):
                     sums = None
                     for s in range(NSEG):
@@ -241,7 +247,6 @@
         out_shape=pltpu.VMEM((LINES, 2, KEPT, ROWS), BF16),
         scratch_shapes=[
             pltpu.VMEM((TILES + 2, ROWS, LANES), F32),
-            pltpu.VMEM((TILES + 2, 2, LINES * STEPS * PIECE, LANES), F32),
             pltpu.VMEM((LINES, 2 * ROWS, WIDE), F32),
         ],
         compiler_params=pltpu.CompilerParams(vmem_limit_bytes=VMEM_LIMIT),

time: 74.3 us -> 74.2 us (level)
  no operation moved by 1% of the time
where the time goes in v7:
time: 74.2 us; the launch traced here: 73.9 us
  blocking collectives  68.5 us (92%)
  Pallas kernels  5.37 us (7%)
    all_to_all x1, blocking collectives, shards(): pieces = lax.all_to_all(white, ('q', 'x', 'r', 'c'), 0, 0, tiled=True)  18.3 us
    all_to_all x1, blocking collectives, shards(): near = lax.all_to_all(spread, ('q', 'x', 'r'), 0, 0, tiled=True)  12.8 us
    all_gather x1, blocking collectives, shards(): both = lax.all_gather(send, 'w', axis=0, tiled=False)  12.6 us
    all_to_all x1, blocking collectives, shards(): parts = lax.all_to_all(lagged, 'y', 0, 0, tiled=True)  11.8 us
    all_gather x1, blocking collectives, shards(): ends = lax.all_gather(picked, 'p', axis=0, tiled=False)  9.37 us
    all_gather x1, blocking collectives, shards(): source = lax.all_gather(near, 'c', axis=0, tiled=False)  3.59 us
    pallas_call x1, Pallas kernels, correlate(): pl.pallas_call(correlate_kernel, in_specs=[vmem] * len(arrays), out_specs...  2.48 us
    pallas_call x1, Pallas kernels, whiten(): pl.pallas_call(whiten_kernel, in_specs=[hbm] * 3, out_specs=[vmem] * 2, o...  1.68 us

profile of v7, /device:TPU:1, one launch (start us, length us, event | category | flops | bytes accessed | tf_op | source)
XLA Modules:
  0.0 73.9 jit_solution(16111789892905180927)
XLA Ops:
  0.0 1.7 %whiten.1 = (bf16[32,16,128]{2,1,0:T(8,128)(2,1)S(1)}, s32[4,16,128]{2,1,0:T(8,128)S(1)}) custom-call(bf16[128,512]{1,0:T(8,128)(2,1)} %bitcast.10, s32[8,16]{1,0:T(8,128)} %bitcast.11, s32[4]{0:T(128)} %plan.1), custom_call_target="tpu_custom_call" | custom-call | tf_op jit(solution)/shard_map/whiten/pallas_call | solution.py:144
  1.7 18.3 %all_to_all.15.gathered = bf16[32,16,128]{2,1,0:T(8,128)(2,1)S(1)} all-to-all(bf16[32,16,128]{2,1,0:T(8,128)(2,1)S(1)} %get-tuple-element.9.white), channel_id=1, replica_groups=mesh['y'=4,'w'=2,'x'=4,'p'=2,'q'=2,'r'=2,'c'=2] {'q','x','r','c'}, dimensions={0} | all-to-all | bytes 262144 | tf_op jit(solution)/shard_map/all_to_all | solution.py:304
  20.0 0.1 pick_near.1
  20.1 9.4 %all-gather = bf16[8,16,128]{2,1,0:T(8,128)(2,1)S(1)} all-gather(bf16[4,16,128]{2,1,0:T(8,128)(2,1)S(1)} %pick_near.1), channel_id=2, replica_groups=mesh['y'=4,'w'=2,'x'=4,'p'=2,'q'=2,'r'=2,'c'=2] {'p'}, dimensions={0}, use_global_device_ids=true | all-gather | bytes 49152 | tf_op jit(solution)/shard_map/all_gather | solution.py:306
  29.5 0.2 pick_far.1
  29.7 12.8 %all_to_all.16 = bf16[16,4,16,128]{3,2,1,0:T(8,128)(2,1)S(1)} all-to-all(bf16[16,4,16,128]{3,2,1,0:T(8,128)(2,1)S(1)} %pick_far.1), channel_id=1, replica_groups=mesh['y'=4,'w'=2,'x'=4,'p'=2,'q'=2,'r'=2,'c'=2] {'q','x','r'}, dimensions={0} | all-to-all | bytes 524288 | tf_op jit(solution)/shard_map/all_to_all | solution.py:308
  42.5 0.0 copy-start
  42.5 3.6 %all-gather.1 = bf16[32,4,16,128]{3,2,1,0:T(8,128)(2,1)S(1)} all-gather(bf16[16,4,16,128]{3,2,1,0:T(8,128)(2,1)S(1)} %all_to_all.16), channel_id=3, replica_groups=mesh['y'=4,'w'=2,'x'=4,'p'=2,'q'=2,'r'=2,'c'=2] {'c'}, dimensions={0}, use_global_device_ids=true | all-gather | bytes 786432 | tf_op jit(solution)/shard_map/all_gather | solution.py:309
  46.1 0.0 copy-done
  46.1 2.5 %correlate.1 = bf16[4,2,208,128]{3,2,1,0:T(8,128)(2,1)S(1)} custom-call(bf16[32,16,128]{2,1,0:T(8,128)(2,1)S(1)} %get-tuple-element.9.white, bf16[2,16,4,16,128]{4,3,2,1,0:T(8,128)(2,1)S(1)} %bitcast.7, bf16[416,512]{1,0:T(8,128)(2,1)S(1)} %copy-done), custom_call_target="tpu_custom_call" | custom-call | tf_op jit(solution)/shard_map/correlate/pallas_call | solution.py:243
  48.5 11.8 %all_to_all.17.parts = bf16[4,2,208,128]{3,2,1,0:T(8,128)(2,1)S(1)} all-to-all(bf16[4,2,208,128]{3,2,1,0:T(8,128)(2,1)S(1)} %correlate.1), channel_id=1, replica_groups=mesh['y'=4,'w'=2,'x'=4,'p'=2,'q'=2,'r'=2,'c'=2] {'y'}, dimensions={0} | all-to-all | bytes 851968 | tf_op jit(solution)/shard_map/all_to_all | solution.py:311
  60.4 0.1 fold.1
  60.4 12.6 %all-gather.2 = bf16[416,128]{1,0:T(8,128)(2,1)S(1)} all-gather(bf16[208,128]{1,0:T(8,128)(2,1)S(1)} %get-tuple-element.12), channel_id=4, replica_groups=mesh['y'=4,'w'=2,'x'=4,'p'=2,'q'=2,'r'=2,'c'=2] {'w'}, dimensions={0}, use_global_device_ids=true | all-gather | bytes 159744 | tf_op jit(solution)/shard_map/all_gather | solution.py:313
  73.1 0.8 %finish.1 = bf16[4,16,2,201]{3,2,1,0:T(2,128)(2,1)} custom-call(f32[208,128]{1,0:T(8,128)S(1)} %get-tuple-element.11.keep, bf16[2,208,128]{2,1,0:T(8,128)(2,1)S(1)} %bitcast.8), custom_call_target="tpu_custom_call" | custom-call | tf_op jit(solution)/shard_map/finish/pallas_call | solution.py:292
Async XLA Ops:
  42.5 3.6 %copy-start = (bf16[416,512]{1,0:T(8,128)(2,1)S(1)}, bf16[416,512]{1,0:T(8,128)(2,1)}, u32[]{:S(2)}) copy-start(bf16[416,512]{1,0:T(8,128)(2,1)} %constant.2.clone.table) | copy-start | bytes 1277956

commit v8 on v7

--- a/solution.py
+++ b/solution.py
@@ -23,6 +23,7 @@
 UNITS = 32
 LINES = 4
 SPREAD = 16
+PARTS = 4
 SLOTS = 2 * STEPS
 KEPT = 208
 LAST = KEPT - SLOTS
@@ -91,11 +92,12 @@
 
 
 def whiten_kernel(records, mask, plan, white, steps, raw_buffer, mask_buffer, plan_buffer, trig, sems):
-    fetches = [
-        pltpu.make_async_copy(records, raw_buffer, sems.at[0]),
-        pltpu.make_async_copy(mask, mask_buffer, sems.at[1]),
-        pltpu.make_async_copy(plan, plan_buffer, sems.at[2]),
-    ]
+    fetches = []
+    for part in range(PARTS):
+        rows = pl.ds(part * (ROWS // PARTS), ROWS // PARTS)
+        fetches.append(pltpu.make_async_copy(records.at[rows], raw_buffer.at[rows], sems.at[part]))
+    fetches.append(pltpu.make_async_copy(mask, mask_buffer, sems.at[PARTS]))
+    fetches.append(pltpu.make_async_copy(plan, plan_buffer, sems.at[PARTS + 1]))
     for fetch in fetches:
         fetch.start()
     row = lax.broadcasted_iota(jnp.int32, (NSEG, FREQ), 0)
@@ -151,7 +153,7 @@
             pltpu.VMEM((NSEG, SB), jnp.int32),
             pltpu.SMEM((STEPS,), jnp.int32),
             pltpu.VMEM((SEGLEN, WIDE), F32),
-            pltpu.SemaphoreType.DMA((3,)),
+            pltpu.SemaphoreType.DMA((PARTS + 2,)),
         ],
         compiler_params=pltpu.CompilerParams(vmem_limit_bytes=VMEM_LIMIT),
         name="whiten",

time: 74.2 us -> 74.1 us (level)
  no operation moved by 1% of the time
where the time goes in v8:
time: 74.1 us; the launch traced here: 73.8 us
  blocking collectives  68.5 us (92%)
  Pallas kernels  5.28 us (7%)
    all_to_all x1, blocking collectives, shards(): pieces = lax.all_to_all(white, ('q', 'x', 'r', 'c'), 0, 0, tiled=True)  18.3 us
    all_to_all x1, blocking collectives, shards(): near = lax.all_to_all(spread, ('q', 'x', 'r'), 0, 0, tiled=True)  12.8 us
    all_gather x1, blocking collectives, shards(): both = lax.all_gather(send, 'w', axis=0, tiled=False)  12.6 us
    all_to_all x1, blocking collectives, shards(): parts = lax.all_to_all(lagged, 'y', 0, 0, tiled=True)  11.9 us
    all_gather x1, blocking collectives, shards(): ends = lax.all_gather(picked, 'p', axis=0, tiled=False)  9.37 us
    all_gather x1, blocking collectives, shards(): source = lax.all_gather(near, 'c', axis=0, tiled=False)  3.59 us
    pallas_call x1, Pallas kernels, correlate(): pl.pallas_call(correlate_kernel, in_specs=[vmem] * len(arrays), out_specs...  2.48 us
    pallas_call x1, Pallas kernels, whiten(): pl.pallas_call(whiten_kernel, in_specs=[hbm] * 3, out_specs=[vmem] * 2, o...  1.6 us

profile of v8, /device:TPU:1, one launch (start us, length us, event | category | flops | bytes accessed | tf_op | source)
XLA Modules:
  0.0 73.8 jit_solution(12452668736561333814)
XLA Ops:
  0.0 1.6 %whiten.1 = (bf16[32,16,128]{2,1,0:T(8,128)(2,1)S(1)}, s32[4,16,128]{2,1,0:T(8,128)S(1)}) custom-call(bf16[128,512]{1,0:T(8,128)(2,1)} %bitcast.10, s32[8,16]{1,0:T(8,128)} %bitcast.11, s32[4]{0:T(128)} %plan.1), custom_call_target="tpu_custom_call" | custom-call | tf_op jit(solution)/shard_map/whiten/pallas_call | solution.py:146
  1.6 18.3 %all_to_all.15.gathered = bf16[32,16,128]{2,1,0:T(8,128)(2,1)S(1)} all-to-all(bf16[32,16,128]{2,1,0:T(8,128)(2,1)S(1)} %get-tuple-element.9.white), channel_id=1, replica_groups=mesh['y'=4,'w'=2,'x'=4,'p'=2,'q'=2,'r'=2,'c'=2] {'q','x','r','c'}, dimensions={0} | all-to-all | bytes 262144 | tf_op jit(solution)/shard_map/all_to_all | solution.py:306
  19.9 0.1 pick_near.1
  20.1 9.4 %all-gather = bf16[8,16,128]{2,1,0:T(8,128)(2,1)S(1)} all-gather(bf16[4,16,128]{2,1,0:T(8,128)(2,1)S(1)} %pick_near.1), channel_id=2, replica_groups=mesh['y'=4,'w'=2,'x'=4,'p'=2,'q'=2,'r'=2,'c'=2] {'p'}, dimensions={0}, use_global_device_ids=true | all-gather | bytes 49152 | tf_op jit(solution)/shard_map/all_gather | solution.py:308
  29.4 0.2 pick_far.1
  29.6 12.8 %all_to_all.16 = bf16[16,4,16,128]{3,2,1,0:T(8,128)(2,1)S(1)} all-to-all(bf16[16,4,16,128]{3,2,1,0:T(8,128)(2,1)S(1)} %pick_far.1), channel_id=1, replica_groups=mesh['y'=4,'w'=2,'x'=4,'p'=2,'q'=2,'r'=2,'c'=2] {'q','x','r'}, dimensions={0} | all-to-all | bytes 524288 | tf_op jit(solution)/shard_map/all_to_all | solution.py:310
  42.4 0.0 copy-start
  42.4 3.6 %all-gather.1 = bf16[32,4,16,128]{3,2,1,0:T(8,128)(2,1)S(1)} all-gather(bf16[16,4,16,128]{3,2,1,0:T(8,128)(2,1)S(1)} %all_to_all.16), channel_id=3, replica_groups=mesh['y'=4,'w'=2,'x'=4,'p'=2,'q'=2,'r'=2,'c'=2] {'c'}, dimensions={0}, use_global_device_ids=true | all-gather | bytes 786432 | tf_op jit(solution)/shard_map/all_gather | solution.py:311
  46.0 0.0 copy-done
  46.0 2.5 %correlate.1 = bf16[4,2,208,128]{3,2,1,0:T(8,128)(2,1)S(1)} custom-call(bf16[32,16,128]{2,1,0:T(8,128)(2,1)S(1)} %get-tuple-element.9.white, bf16[2,16,4,16,128]{4,3,2,1,0:T(8,128)(2,1)S(1)} %bitcast.7, bf16[416,512]{1,0:T(8,128)(2,1)S(1)} %copy-done), custom_call_target="tpu_custom_call" | custom-call | tf_op jit(solution)/shard_map/correlate/pallas_call | solution.py:245
  48.5 11.9 %all_to_all.17.parts = bf16[4,2,208,128]{3,2,1,0:T(8,128)(2,1)S(1)} all-to-all(bf16[4,2,208,128]{3,2,1,0:T(8,128)(2,1)S(1)} %correlate.1), channel_id=1, replica_groups=mesh['y'=4,'w'=2,'x'=4,'p'=2,'q'=2,'r'=2,'c'=2] {'y'}, dimensions={0} | all-to-all | bytes 851968 | tf_op jit(solution)/shard_map/all_to_all | solution.py:313
  60.3 0.1 fold.1
  60.4 12.6 %all-gather.2 = bf16[416,128]{1,0:T(8,128)(2,1)S(1)} all-gather(bf16[208,128]{1,0:T(8,128)(2,1)S(1)} %get-tuple-element.12), channel_id=4, replica_groups=mesh['y'=4,'w'=2,'x'=4,'p'=2,'q'=2,'r'=2,'c'=2] {'w'}, dimensions={0}, use_global_device_ids=true | all-gather | bytes 159744 | tf_op jit(solution)/shard_map/all_gather | solution.py:315
  73.0 0.8 %finish.1 = bf16[4,16,2,201]{3,2,1,0:T(2,128)(2,1)} custom-call(f32[208,128]{1,0:T(8,128)S(1)} %get-tuple-element.11.keep, bf16[2,208,128]{2,1,0:T(8,128)(2,1)S(1)} %bitcast.8), custom_call_target="tpu_custom_call" | custom-call | tf_op jit(solution)/shard_map/finish/pallas_call | solution.py:294
Async XLA Ops:
  42.4 3.6 %copy-start = (bf16[416,512]{1,0:T(8,128)(2,1)S(1)}, bf16[416,512]{1,0:T(8,128)(2,1)}, u32[]{:S(2)}) copy-start(bf16[416,512]{1,0:T(8,128)(2,1)} %constant.2.clone.table) | copy-start | bytes 1277956

commit v9 on v7

--- a/solution.py
+++ b/solution.py
@@ -86,8 +86,13 @@
     return matrix, count.astype(F32)
 
 
-def unit_of(tile, pair):
-    return (pair // LINES) * (TILES * LINES) + tile * LINES + pair % LINES
+def crossed(pair):
+    end = lax.axis_index("p")
+    return pair + (end if pair % 2 == 0 else -end)
+
+
+def slot_of(tile, pair):
+    return (pair // LINES) * (TILES * LINES) + tile * LINES + crossed(pair % LINES)
 
 
 def whiten_kernel(records, mask, plan, white, steps, raw_buffer, mask_buffer, plan_buffer, trig, sems):
@@ -133,7 +138,7 @@
         lanes = slice((tile % 2) * LANES, (tile % 2 + 1) * LANES)
         part = (spec_part[:, lanes] * weight[:, lanes]).astype(BF16)
         for group in range(ROWS // PIECE):
-            white[unit_of(tile, group)] = part[group * PIECE : (group + 1) * PIECE]
+            white[slot_of(tile, group)] = part[group * PIECE : (group + 1) * PIECE]
     for k in range(STEPS):
         steps[k] = jnp.full((PIECE, LANES), plan_buffer[k], jnp.int32)
 
@@ -202,9 +207,8 @@
 
 def correlate_kernel(white, source, table, lagged, own, cross):
     for tile in range(TILES):
-        for q in range(2):
-            units = white[pl.ds(unit_of(tile, q * LINES), LINES)].astype(F32)
-            own[tile, pl.ds(q * (LINES * PIECE), LINES * PIECE), :] = units.reshape(LINES * PIECE, LANES)
+        for pair in range(ROWS // PIECE):
+            own[tile, pl.ds(pair * PIECE, PIECE), :] = white[slot_of(tile, pair)].astype(F32)
     for half in range(2):
         own[TILES + half] = own[half] + own[half + 2]
 
@@ -234,7 +238,7 @@
         out = both[:KEPT] + (both[KEPT:] + mm_rows(table[pl.ds(0, KEPT), :], low))
         for core in range(2):
             part = out[:, core * ROWS : (core + 1) * ROWS]
-            lagged[line, core] = pack(part, part[LAST:])
+            lagged[line, crossed(core)] = pack(part, part[LAST:])
 
 
 def correlate(*arrays):
@@ -303,7 +307,7 @@
     white, steps = whiten(records.reshape(ROWS, SEGLEN), masks[0].T, plan)
     pieces = lax.all_to_all(white, ("q", "x", "r", "c"), 0, 0, tiled=True)
     picked = pick(pick_near_kernel, steps, pieces, (STEPS, PIECE, LANES), "pick_near")
-    ends = lax.all_gather(picked, "p", axis=0, tiled=False)
+    ends = lax.all_gather(picked, ("p", "c"), axis=0, tiled=False, axis_index_groups=[[0, 3], [1, 2]])
     spread = pick(pick_far_kernel, steps, ends, (SPREAD, STEPS, PIECE, LANES), "pick_far")
     near = lax.all_to_all(spread, ("q", "x", "r"), 0, 0, tiled=True)
     source = lax.all_gather(near, "c", axis=0, tiled=False)

time: 74.2 us -> 74.3 us (level)
  no operation moved by 1% of the time
where the time goes in v9:
time: 74.3 us; the launch traced here: 74 us
  blocking collectives  68.6 us (92%)
  Pallas kernels  5.38 us (7%)
    all_to_all x1, blocking collectives, shards(): pieces = lax.all_to_all(white, ('q', 'x', 'r', 'c'), 0, 0, tiled=True)  18.3 us
    all_to_all x1, blocking collectives, shards(): near = lax.all_to_all(spread, ('q', 'x', 'r'), 0, 0, tiled=True)  12.7 us
    all_gather x1, blocking collectives, shards(): both = lax.all_gather(send, 'w', axis=0, tiled=False)  12.5 us
    all_to_all x1, blocking collectives, shards(): parts = lax.all_to_all(lagged, 'y', 0, 0, tiled=True)  11.8 us
    all_gather x1, blocking collectives, shards(): lax.all_gather(picked, ('p', 'c'), axis=0, tiled=False, axis_index_groups...  9.57 us
    all_gather x1, blocking collectives, shards(): source = lax.all_gather(near, 'c', axis=0, tiled=False)  3.68 us
    pallas_call x1, Pallas kernels, correlate(): pl.pallas_call(correlate_kernel, in_specs=[vmem] * len(arrays), out_specs...  2.5 us
    pallas_call x1, Pallas kernels, whiten(): pl.pallas_call(whiten_kernel, in_specs=[hbm] * 3, out_specs=[vmem] * 2, o...  1.68 us

profile of v9, /device:TPU:1, one launch (start us, length us, event | category | flops | bytes accessed | tf_op | source)
XLA Modules:
  0.0 74.0 jit_solution(2001290396837476444)
XLA Ops:
  0.0 1.7 %whiten.1 = (bf16[32,16,128]{2,1,0:T(8,128)(2,1)S(1)}, s32[4,16,128]{2,1,0:T(8,128)S(1)}) custom-call(bf16[128,512]{1,0:T(8,128)(2,1)} %bitcast.10, s32[8,16]{1,0:T(8,128)} %bitcast.11, s32[4]{0:T(128)} %plan.1), custom_call_target="tpu_custom_call" | custom-call | tf_op jit(solution)/shard_map/whiten/pallas_call | solution.py:149
  1.7 18.3 %all_to_all.15.gathered = bf16[32,16,128]{2,1,0:T(8,128)(2,1)S(1)} all-to-all(bf16[32,16,128]{2,1,0:T(8,128)(2,1)S(1)} %get-tuple-element.9.white), channel_id=1, replica_groups=mesh['y'=4,'w'=2,'x'=4,'p'=2,'q'=2,'r'=2,'c'=2] {'q','x','r','c'}, dimensions={0} | all-to-all | bytes 262144 | tf_op jit(solution)/shard_map/all_to_all | solution.py:308
  20.0 0.1 pick_near.1
  20.1 9.6 %all-gather = bf16[8,16,128]{2,1,0:T(8,128)(2,1)S(1)} all-gather(bf16[4,16,128]{2,1,0:T(8,128)(2,1)S(1)} %pick_near.1), channel_id=2, replica_groups={{0,9},{1,8},{2,11},{3,10},{4,13},{5,12},{6,15},{7,14},{16,25},{17,24},{..., dimensions={0}, use_global_device_ids=true | all-gather | bytes 49152 | tf_op jit(solution)/shard_map/all_gather | solution.py:310
  29.7 0.2 pick_far.1
  29.9 12.7 %all_to_all.16 = bf16[16,4,16,128]{3,2,1,0:T(8,128)(2,1)S(1)} all-to-all(bf16[16,4,16,128]{3,2,1,0:T(8,128)(2,1)S(1)} %pick_far.1), channel_id=1, replica_groups=mesh['y'=4,'w'=2,'x'=4,'p'=2,'q'=2,'r'=2,'c'=2] {'q','x','r'}, dimensions={0} | all-to-all | bytes 524288 | tf_op jit(solution)/shard_map/all_to_all | solution.py:312
  42.6 0.0 copy-start
  42.6 3.7 %all-gather.1 = bf16[32,4,16,128]{3,2,1,0:T(8,128)(2,1)S(1)} all-gather(bf16[16,4,16,128]{3,2,1,0:T(8,128)(2,1)S(1)} %all_to_all.16), channel_id=3, replica_groups=mesh['y'=4,'w'=2,'x'=4,'p'=2,'q'=2,'r'=2,'c'=2] {'c'}, dimensions={0}, use_global_device_ids=true | all-gather | bytes 786432 | tf_op jit(solution)/shard_map/all_gather | solution.py:313
  46.3 0.0 copy-done
  46.3 2.5 %correlate.1 = bf16[4,2,208,128]{3,2,1,0:T(8,128)(2,1)S(1)} custom-call(bf16[32,16,128]{2,1,0:T(8,128)(2,1)S(1)} %get-tuple-element.9.white, bf16[2,16,4,16,128]{4,3,2,1,0:T(8,128)(2,1)S(1)} %bitcast.7, bf16[416,512]{1,0:T(8,128)(2,1)S(1)} %copy-done), custom_call_target="tpu_custom_call" | custom-call | tf_op jit(solution)/shard_map/correlate/pallas_call | solution.py:247
  48.8 11.8 %all_to_all.17.parts = bf16[4,2,208,128]{3,2,1,0:T(8,128)(2,1)S(1)} all-to-all(bf16[4,2,208,128]{3,2,1,0:T(8,128)(2,1)S(1)} %correlate.1), channel_id=1, replica_groups=mesh['y'=4,'w'=2,'x'=4,'p'=2,'q'=2,'r'=2,'c'=2] {'y'}, dimensions={0} | all-to-all | bytes 851968 | tf_op jit(solution)/shard_map/all_to_all | solution.py:315
  60.6 0.1 fold.1
  60.7 12.5 %all-gather.2 = bf16[416,128]{1,0:T(8,128)(2,1)S(1)} all-gather(bf16[208,128]{1,0:T(8,128)(2,1)S(1)} %get-tuple-element.12), channel_id=4, replica_groups=mesh['y'=4,'w'=2,'x'=4,'p'=2,'q'=2,'r'=2,'c'=2] {'w'}, dimensions={0}, use_global_device_ids=true | all-gather | bytes 159744 | tf_op jit(solution)/shard_map/all_gather | solution.py:317
  73.2 0.8 %finish.1 = bf16[4,16,2,201]{3,2,1,0:T(2,128)(2,1)} custom-call(f32[208,128]{1,0:T(8,128)S(1)} %get-tuple-element.11.keep, bf16[2,208,128]{2,1,0:T(8,128)(2,1)S(1)} %bitcast.8), custom_call_target="tpu_custom_call" | custom-call | tf_op jit(solution)/shard_map/finish/pallas_call | solution.py:296
Async XLA Ops:
  42.6 3.7 %copy-start = (bf16[416,512]{1,0:T(8,128)(2,1)S(1)}, bf16[416,512]{1,0:T(8,128)(2,1)}, u32[]{:S(2)}) copy-start(bf16[416,512]{1,0:T(8,128)(2,1)} %constant.2.clone.table) | copy-start | bytes 1277956
